TPU v7x, 1024 devices: a whole 4x4x32 slice. The times are simulated.
1024 devices in a mesh: resp: 4 (over x), ep: 32 (over y, z_lo), kv: 8 (over z_hi, core).
Axes of the slice: x: 4, y: 4, z: 32 (z_hi: 4, z_lo: 8; z = z_hi * 8 + z_lo), core: 2. Of those that a mesh axis runs over, the one named last changes fastest.
Arguments:
- lengths: int32 [4], replicated, may hold values from 1 to 4096, 8192 in all
- queries: bfloat16 [4, 4096, 4096], P('resp', 'ep'), may hold values from -140 to 140
- grad_out: bfloat16 [4, 4096, 4096], P('resp', 'ep'), may hold values from -6 to 6
- prompt_keys: bfloat16 [1024, 256], P(('ep', 'kv')), may hold values from -7 to 7
- prompt_values: bfloat16 [1024, 256], P(('ep', 'kv')), may hold values from -6 to 6
Outputs:
- grad_queries: float32 [4, 4096, 4096], P('resp', 'ep', 'kv')
- grad_keys: float32 [1024, 256], P(('ep', 'kv'))
- grad_values: float32 [1024, 256], P(('ep', 'kv'))
Inputs may be any that keep to these rules, and one draw needn't show every extreme that they name: `lengths`: the longest response fills all 4096 slots.
All inputs are finite; a program needn't handle non-finite values.
Results may differ from a plain program's by a relative error of at most 0.0029.
Values may be sent and summed in bfloat16 or wider, within the bound.
A program may use at most 32 MiB of HBM per device.

v0:
```python
import math

import jax
import jax.numpy as jnp
from jax import lax
from jax.sharding import PartitionSpec as P

HQ = 32
KVH = 2
HD = 128


def combined_all(part, axis, combine):
    gathered = jax.tree.map(lambda a: lax.all_gather(a, axis), part)

    def take(source):
        return jax.tree.map(lambda a: lax.dynamic_index_in_dim(a, source, 0, False), gathered)

    return lax.fori_loop(
        1, lax.axis_size(axis), lambda source, state: combine(state, take(source)), take(0)
    )


def combine_pair(first, second):
    top = jnp.maximum(first[0], second[0])
    return (top, first[1] * jnp.exp(first[0] - top) + second[1] * jnp.exp(second[0] - top))


def body(lengths, queries, grad_out, prompt_keys, prompt_values):
    rows = queries.shape[1]
    width = queries.shape[2]
    groups = HQ // KVH
    score_scale = 1.0 / math.sqrt(HD)
    resp_index = lax.axis_index("resp")
    ep_index = lax.axis_index("ep")
    own_length = jnp.sum(
        jnp.where(jnp.arange(lengths.shape[0], dtype=jnp.int32) == resp_index, lengths, 0)
    )
    positions = ep_index * rows + jnp.arange(rows, dtype=jnp.int32)
    valid = positions < own_length
    masked = jnp.where(valid[:, None], grad_out[0], jnp.zeros((), grad_out.dtype))
    key_rows, value_rows = (
        lax.all_gather(prompt_keys, "ep", axis=0, tiled=True),
        lax.all_gather(prompt_values, "ep", axis=0, tiled=True),
    )
    span = key_rows.shape[0]
    query_four = queries[0].reshape(rows, KVH, groups, HD)
    cotan_four = masked.reshape(rows, KVH, groups, HD)
    key_three = key_rows.reshape(span, KVH, HD)
    value_three = value_rows.reshape(span, KVH, HD)

    def head_scores(head):
        scores = (
            jnp.einsum(
                "rgd,pd->rgp",
                query_four[:, head],
                key_three[:, head],
                preferred_element_type=jnp.float32,
            )
            * score_scale
        )
        dprob = jnp.einsum(
            "rgd,pd->rgp",
            cotan_four[:, head],
            value_three[:, head],
            preferred_element_type=jnp.float32,
        )
        return (scores, dprob)

    local_top = []
    local_total = []
    local_inner = []
    for head in range(KVH):
        scores, dprob = head_scores(head)
        top = jnp.max(scores, axis=-1)
        expo = jnp.exp(scores - top[..., None])
        local_top.append(top)
        local_total.append(jnp.sum(expo, axis=-1))
        local_inner.append(jnp.sum(expo * dprob, axis=-1))
    local_top = jnp.stack(local_top, axis=1)
    local_total = jnp.stack(local_total, axis=1)
    local_inner = jnp.stack(local_inner, axis=1)
    glob_top, glob_total = combined_all((local_top, local_total), "kv", combine_pair)
    glob_inner = lax.psum(local_inner * jnp.exp(local_top - glob_top), "kv")
    delta = glob_inner / glob_total
    grad_q_heads = []
    grad_k_heads = []
    grad_v_heads = []
    for head in range(KVH):
        scores, dprob = head_scores(head)
        prob = jnp.exp(scores - glob_top[:, head, :, None]) / glob_total[:, head, :, None]
        dscore = (prob * (dprob - delta[:, head, :, None])).astype(jnp.bfloat16)
        prob_low = prob.astype(jnp.bfloat16)
        grad_q_heads.append(
            jnp.einsum(
                "rgp,pd->rgd", dscore, key_three[:, head], preferred_element_type=jnp.float32
            )
            * score_scale
        )
        grad_k_heads.append(
            jnp.einsum(
                "rgp,rgd->pd", dscore, query_four[:, head], preferred_element_type=jnp.float32
            )
            * score_scale
        )
        grad_v_heads.append(
            jnp.einsum(
                "rgp,rgd->pd", prob_low, cotan_four[:, head], preferred_element_type=jnp.float32
            )
        )
    grad_q = jnp.stack(grad_q_heads, axis=1).reshape(rows, width)
    grad_k = jnp.stack(grad_k_heads, axis=1).reshape(span, KVH * HD)
    grad_v = jnp.stack(grad_v_heads, axis=1).reshape(span, KVH * HD)
    grad_q_own = lax.psum_scatter(grad_q, "kv", scatter_dimension=1, tiled=True)
    summed_k, summed_v = lax.psum((grad_k, grad_v), "resp")
    owned_k, owned_v = (
        lax.psum_scatter(summed_k, "ep", scatter_dimension=0, tiled=True),
        lax.psum_scatter(summed_v, "ep", scatter_dimension=0, tiled=True),
    )
    return (grad_q_own[None], owned_k, owned_v)


def solution(mesh):
    return jax.shard_map(
        body,
        mesh=mesh,
        in_specs=(
            P(),
            P("resp", "ep", None),
            P("resp", "ep", None),
            P(("ep", "kv"), None),
            P(("ep", "kv"), None),
        ),
        out_specs=(P("resp", "ep", "kv"), P(("ep", "kv"), None), P(("ep", "kv"), None)),
        check_vma=False,
    )
```

profile of v0, /device:TPU:32, one launch (start us, length us, event | category | flops | bytes accessed | tf_op | source)
XLA Modules:
  0.0 906.5 jit_solution(9429996053786997218)
XLA Ops:
  8.1 1.7 copy.50
  9.8 124.4 %all-gather.2 = bf16[32,4,256]{2,1,0:T(4,128)(2,1)S(1)} all-gather(bf16[1,4,256]{2,1,0:T(4,128)(2,1)S(1)} %bitcast.159), channel_id=1, replica_groups=mesh['resp'=4,'ep'=32,'kv'=8] {'ep'}, dimensions={0}, use_global_device_ids=true | all-gather | bytes 67584 | tf_op jit(solution)/shard_map/all_gather | solution.py:43
  134.4 0.7 copy.57
  135.1 1.3 copy.58
  136.4 112.9 %all-gather.3 = bf16[32,4,256]{2,1,0:T(4,128)(2,1)S(1)} all-gather(bf16[1,4,256]{2,1,0:T(4,128)(2,1)S(1)} %bitcast.160), channel_id=1, replica_groups=mesh['resp'=4,'ep'=32,'kv'=8] {'ep'}, dimensions={0}, use_global_device_ids=true | all-gather | bytes 67584 | tf_op jit(solution)/shard_map/all_gather | solution.py:44
  250.7 0.7 add_compare_fusion
  251.3 1.4 broadcast_select_fusion
  252.7 1.4 fusion.6
  254.1 1.3 fusion.7
  255.4 37.2 %all-gather.1 = f32[1024,2,16]{0,2,1:T(8,128)S(1)} all-gather(f32[128,2,16]{0,2,1:T(8,128)S(1)} %pad_maximum_fusion.4), channel_id=3, replica_groups=mesh['resp'=4,'ep'=32,'kv'=8] {'kv'}, dimensions={0}, use_global_device_ids=true | all-gather | bytes 147456 | tf_op jit(solution)/shard_map/all_gather | solution.py:14
  292.6 27.9 %all-gather = f32[1024,2,16]{0,2,1:T(8,128)S(1)} all-gather(f32[128,2,16]{0,2,1:T(8,128)S(1)} %pad_maximum_fusion.3), channel_id=2, replica_groups=mesh['resp'=4,'ep'=32,'kv'=8] {'kv'}, dimensions={0}, use_global_device_ids=true | all-gather | bytes 147456 | tf_op jit(solution)/shard_map/all_gather | solution.py:14
  321.1 1.5 convolution_bitcast_fusion.1
  323.1 0.8 copy.75
  323.9 58.1 %psum.21 = f32[128,2,16]{0,2,1:T(8,128)S(1)} all-reduce(f32[128,2,16]{0,2,1:T(8,128)S(1)} %maximum_multiply_fusion), channel_id=1, replica_groups=mesh['resp'=4,'ep'=32,'kv'=8] {'kv'}, use_global_device_ids=true, to_apply=%region_9.10 | all-reduce | flops 4096 | bytes 32768 | tf_op jit(solution)/shard_map/psum | solution.py:84
  382.0 1.6 multiply_convert_fusion.1
  384.6 0.8 copy.70
  385.4 1.4 fusion.1
  386.8 1.4 fusion
  388.4 1.9 copy.65
  390.3 1.3 dynamic-slice
  392.2 494.3 %all-reduce.6.cloned.1.call-done = (f32[128,256]{1,0:T(8,128)}, f32[128,256]{1,0:T(8,128)}) async-done(((f32[128,256]{1,0:T(8,128)}, f32[128,256]{1,0:T(8,128)}), (f32[128,256]{1,0:T(8,128)}, f32[128,256]{1,0:T(8,128)})) %all-reduce.6.cloned.1.call-update) | async-done | bytes 262160
  886.6 0.7 constant_dynamic-slice_fusion.2
  887.3 0.7 constant_dynamic-slice_fusion.3
  888.0 11.1 %all-reduce.3 = (f32[4,256]{1,0:T(4,128)}, f32[4,256]{1,0:T(4,128)}) all-reduce(f32[4,256]{1,0:T(4,128)S(1)} %constant_dynamic-slice_fusion.3, f32[4,256]{1,0:T(4,128)S(1)} %constant_dynamic-slice_fusion.2), channel_id=1, replica_groups=mesh['resp'=4,'ep'=32,'kv'=8] {'resp'}, use_global_device_ids=true, to_apply=%region_11.12 | all-reduce | flops 2048 | bytes 16384 | tf_op jit(solution)/shard_map/psum | solution.py:115
  (70 shorter events, 4.1 us)
Async XLA Ops:
  8.0 1.8 copy-start.10
  8.0 126.4 %copy-start.5 = (bf16[1,128,4096]{2,1,0:T(8,128)(2,1)S(1)}, bf16[1,128,4096]{2,1,0:T(8,128)(2,1)}, u32[]{:S(2)}) copy-start(bf16[1,128,4096]{2,1,0:T(8,128)(2,1)} %param.9) | copy-start | bytes 3145732
  8.0 878.6 %all-reduce.6.cloned.1.call-start = ((), (), s32[]{:S(2)}) async-start(), calls=%async_computation.2 | async-start | bytes 524288
  134.3 115.1 %copy-start.6 = (bf16[128,1,128]{2,1,0:T(2,128)(2,1)}, bf16[128,1,128]{2,1,0:T(2,128)(2,1)S(1)}, u32[]{:S(2)}) copy-start(bf16[128,1,128]{2,1,0:T(2,128)(2,1)S(1)} %get-tuple-element.177) | copy-start | bytes 98308
  134.4 2.0 copy-start.11
  136.4 113.6 %copy-start.12 = (s32[4]{0:T(128)S(1)}, s32[4]{0:T(128)}, u32[]{:S(2)}) copy-start(s32[4]{0:T(128)} %param.7) | copy-start | bytes 52
  252.7 2.7 copy-start
  321.1 1.6 copy-start.8
  321.1 1.6 copy-start.9
  321.1 1.6 copy-start.1
  382.0 1.9 copy-start.2
  383.6 0.9 copy-start.3
  383.9 1.5 copy-start.7
  384.2 1.1 copy-start.4
  385.4 513.7 %reduce-scatter.2.cloned.1.call-start = ((), (), s32[]{:S(2)}) async-start(), calls=%async_computation.1 | async-start | bytes 2359296 | tf_op jit(solution)/shard_map/reduce_scatter | solution.py:114
Sparse Core Ops, SparseCore 0:
  385.5 501.0 all-reduce.5
Sparse Core Ops, SparseCore 1:
  390.4 114.8 reduce-scatter.1
where the time goes:
time: 907 us
  waiting for transfers between devices  494 us (54%)
  blocking collectives  372 us (41%)
  between operations  16.5 us (2%)
  local copies, waits for them, and re-layouts  10.4 us (1%)
    unnamed x3, waiting for transfers between devices  494 us
    all_gather x1, blocking collectives, body(): lax.all_gather(prompt_keys, 'ep', axis=0, tiled=True)  124 us
    all_gather x1, blocking collectives, body(): lax.all_gather(prompt_values, 'ep', axis=0, tiled=True)  113 us
    all_gather x2, blocking collectives, combined_all(): gathered = jax.tree.map(lambda a: lax.all_gather(a, axis), part)  65 us
    psum x1, blocking collectives, body(): glob_inner = lax.psum(local_inner * jnp.exp(local_top - glob_top), 'kv')  58.1 us
  transfers between devices with their start and end apart: 2, of which 1 were waited for; matrix products, arithmetic and copies ran while one was open for 1% of the time, Pallas kernels for 0%

commit v1 on v0

v1 whole, which is shorter than its diff:
```python
import functools
import math

import jax
import jax.numpy as jnp
from jax import lax
from jax.experimental import pallas as pl
from jax.experimental.pallas import tpu as pltpu
from jax.sharding import PartitionSpec as P

HD = 128
KVH = 2
CORES = 2
NY = 4
MESH = pl.DeviceIdType.MESH
BF16 = jnp.bfloat16
F32 = jnp.float32


def kernel(
    geo,
    len_ref,
    q_hbm,
    g_hbm,
    k_ref,
    v_ref,
    gq_hbm,
    gk_ref,
    gv_ref,
    q_v,
    g_v,
    swap_tx,
    swap_rx,
    pack_f,
    pack,
    near,
    kv,
    p_t,
    ds_t,
    acc,
    acc_rx,
    pl_tx,
    pl_rx,
    z_tx,
    z_rx,
    x_tx,
    x_rx,
    gq_v,
    in_sem,
    out_sem,
    swap_ss,
    swap_rs,
    near_ss,
    near_rs,
    gat_ss,
    gat_rs,
    sib_ss,
    sib_rs,
    acc_ss,
    acc_rs,
    pl_ss,
    pl_rs,
    z_ss,
    z_rs,
    x_ss,
    x_rs,
):
    nx, ny, zl, zh = geo
    nz = zl * zh
    half = nz // KVH
    nt = half // nx
    plane = nx * ny
    rows = q_v.shape[0]
    width = q_v.shape[1]
    heads = width // HD
    blk = kv.shape[3]
    span = CORES * plane * blk
    scale = 1.0 / math.sqrt(HD)

    x = lax.axis_index("resp")
    ep = lax.axis_index("ep")
    kvi = lax.axis_index("kv")
    y, z_lo = lax.div(ep, zl), lax.rem(ep, zl)
    z_hi, c = lax.div(kvi, CORES), lax.rem(kvi, CORES)
    z = z_hi * zl + z_lo
    me = x * ny + y
    sib = 1 - c
    zhalf = lax.div(z, half)

    def dev(xx, yy, zz, cc):
        return (xx, yy * zl + lax.rem(zz, zl), lax.div(zz, zl) * CORES + cc)

    def rcopy(src, dst, ss, rs, device):
        return pltpu.make_async_remote_copy(
            src_ref=src, dst_ref=dst, send_sem=ss, recv_sem=rs, device_id=device, device_id_type=MESH
        )

    def to_z(i):
        return half * c + nx * i + lax.rem(z + x, nx)

    def from_z(i):
        return half * c + nx * i + lax.rem(z - x + nx, nx)

    def plane_dev(slot):
        return dev(lax.div(slot, ny), lax.rem(slot, ny), z, c)

    my_t = lax.div(lax.rem(z, half), nx)
    sib_dev = dev(x, y, z, sib)

    q_in = pltpu.make_async_copy(
        q_hbm.at[0, :, pl.ds(pl.multiple_of(kvi * width, width), width)], q_v, in_sem.at[0]
    )
    g_in = pltpu.make_async_copy(
        g_hbm.at[0, :, pl.ds(pl.multiple_of(kvi * width, width), width)], g_v, in_sem.at[1]
    )
    q_in.start()
    g_in.start()

    barrier = pltpu.get_barrier_semaphore()

    def signal(device):
        pl.semaphore_signal(barrier, inc=1, device_id=device, device_id_type=MESH)

    signal(sib_dev)

    def signal_plane(o, carry):
        signal(plane_dev(lax.rem(me + o, plane)))
        return carry

    lax.fori_loop(1, plane, signal_plane, 0)

    def signal_x(o, carry):
        signal(dev(lax.rem(x + o, nx), y, z, sib))
        return carry

    lax.fori_loop(1, nx, signal_x, 0)

    def is_self(zz):
        return jnp.logical_and(zz == z, zhalf == c)

    def signal_z(i, carry):
        @pl.when(jnp.logical_not(is_self(to_z(i))))
        def _():
            signal(dev(x, y, to_z(i), zhalf))

        @pl.when(jnp.logical_not(is_self(from_z(i))))
        def _():
            signal(dev(x, y, from_z(i), zhalf))

        return carry

    lax.fori_loop(0, nt, signal_z, 0)
    has_self = jnp.logical_and(x == 0, zhalf == c)
    total = 1 + (plane - 1) + (nx - 1) + 2 * nt
    pl.semaphore_wait(barrier, total - jnp.where(has_self, 2, 0))

    def head_of(ref, h):
        value = ref[...].astype(F32)
        return jnp.where(h == 0, value[:, :HD], value[:, HD:])

    lanes = k_ref.shape[0]
    swap_tx[0:lanes] = head_of(k_ref, sib)
    swap_tx[lanes:] = head_of(v_ref, sib)
    swap = rcopy(swap_tx, swap_rx, swap_ss, swap_rs, sib_dev)
    swap.start()
    pack_f[pl.ds(lanes * c, lanes)] = head_of(k_ref, c)
    pack_f[pl.ds(lanes * (2 + c), lanes)] = head_of(v_ref, c)
    swap.wait()
    pack_f[pl.ds(lanes * sib, lanes)] = swap_rx[0:lanes]
    pack_f[pl.ds(lanes * (2 + sib), lanes)] = swap_rx[lanes:]
    pack[...] = pack_f[...].astype(BF16)

    def near_copy(i):
        return rcopy(pack, near.at[my_t], near_ss.at[i], near_rs.at[my_t], dev(x, y, to_z(i), zhalf))

    def near_send(i, carry):
        own = is_self(to_z(i))

        @pl.when(own)
        def _():
            near[my_t] = pack[...]

        @pl.when(jnp.logical_not(own))
        def _():
            near_copy(i).start()

        return carry

    lax.fori_loop(0, nt, near_send, 0)

    def near_recv(i, carry):
        @pl.when(jnp.logical_not(is_self(from_z(i))))
        def _():
            rcopy(pack, near.at[i], near_ss.at[0], near_rs.at[i], sib_dev).wait_recv()

        return carry

    lax.fori_loop(0, nt, near_recv, 0)

    got = near[...].astype(F32).reshape(nt, 2, 2 * lanes, HD)
    kv[c, me, 0] = got[:, 0].reshape(blk, HD).astype(BF16)
    kv[c, me, 1] = got[:, 1].reshape(blk, HD).astype(BF16)

    def gather_send(o, carry):
        rcopy(
            kv.at[c, me],
            kv.at[c, me],
            gat_ss.at[o],
            gat_rs.at[me],
            plane_dev(lax.rem(me + o, plane)),
        ).start()
        return carry

    lax.fori_loop(1, plane, gather_send, 0)

    def gather_recv(o, carry):
        slot = lax.rem(me - o + plane, plane)
        rcopy(kv.at[c, me], kv.at[c, slot], gat_ss.at[0], gat_rs.at[slot], sib_dev).wait_recv()
        return carry

    lax.fori_loop(1, plane, gather_recv, 0)
    share = rcopy(kv.at[c], kv.at[c], sib_ss, sib_rs, sib_dev)
    share.start()
    share.wait_send()
    rcopy(kv.at[sib], kv.at[sib], sib_ss, sib_rs, sib_dev).wait_recv()

    q_in.wait()
    g_in.wait()

    keys = kv[:, :, 0].reshape(span, HD)
    values = kv[:, :, 1].reshape(span, HD)
    own_length = len_ref[x]
    valid = ep * rows + lax.broadcasted_iota(jnp.int32, (rows, HD), 0) < own_length
    factor = scale * math.log2(math.e)
    for h in range(heads):
        cols = slice(h * HD, (h + 1) * HD)
        g_v[:, cols] = jnp.where(valid, g_v[:, cols], jnp.zeros((), BF16))
        q_h = q_v[:, cols]
        g_h = g_v[:, cols]
        s = lax.dot_general(keys, q_h, (((1,), (1,)), ((), ())), preferred_element_type=F32)
        top = jnp.max(s, axis=0, keepdims=True)
        e = jnp.exp2((s - top) * factor)
        prob = e * (1.0 / jnp.sum(e, axis=0, keepdims=True))
        p_t[:, h * rows : (h + 1) * rows] = prob.astype(BF16)
        dp = lax.dot_general(values, g_h, (((1,), (1,)), ((), ())), preferred_element_type=F32)
        delta = jnp.sum(prob * dp, axis=0, keepdims=True)
        ds_t[:, h * rows : (h + 1) * rows] = (prob * (dp - delta)).astype(BF16)

    def stacked(ref):
        return jnp.concatenate([ref[:, h * HD : (h + 1) * HD] for h in range(heads)], axis=0)

    acc[1] = jnp.dot(p_t[...], stacked(g_v), preferred_element_type=F32).reshape(CORES, span // 2, HD)
    acc_v = rcopy(acc.at[1, sib], acc_rx.at[1], acc_ss.at[1], acc_rs.at[1], sib_dev)
    acc_v.start()
    acc[0] = jnp.dot(ds_t[...], stacked(q_v), preferred_element_type=F32).reshape(CORES, span // 2, HD)
    acc_k = rcopy(acc.at[0, sib], acc_rx.at[0], acc_ss.at[0], acc_rs.at[0], sib_dev)
    acc_k.start()

    def plane_send(part):
        both = (acc[part, c] + acc_rx[part]).astype(BF16)
        pl_tx[part] = both.reshape(plane, blk, HD)
        pl_rx[part, me] = pl_tx[part, me]

        def send(o, carry):
            to = lax.rem(me + o, plane)
            rcopy(
                pl_tx.at[part, to], pl_rx.at[part, me], pl_ss.at[part, o], pl_rs.at[part, me], plane_dev(to)
            ).start()
            return carry

        lax.fori_loop(1, plane, send, 0)

    acc_v.wait()
    plane_send(1)
    acc_k.wait()
    plane_send(0)

    keys_t = keys.T
    gq_t = jnp.dot(keys_t, ds_t[...], preferred_element_type=F32) * scale
    for h in range(heads):
        gq_v[:, h * HD : (h + 1) * HD] = gq_t[:, h * rows : (h + 1) * rows].T
    gq_out = pltpu.make_async_copy(gq_v, gq_hbm.at[0], out_sem)
    gq_out.start()

    def plane_recv(part):
        def recv(o, carry):
            slot = lax.rem(me - o + plane, plane)
            rcopy(
                pl_tx.at[part, slot], pl_rx.at[part, slot], pl_ss.at[part, 0], pl_rs.at[part, slot], sib_dev
            ).wait_recv()
            return carry

        lax.fori_loop(1, plane, recv, 0)
        return jnp.sum(pl_rx[part].astype(F32), axis=0).reshape(nt, 1, 2 * lanes, HD)

    v_sum = plane_recv(1)
    k_sum = plane_recv(0)
    z_tx[...] = jnp.concatenate([k_sum, v_sum], axis=1).reshape(nt, 4 * lanes, HD).astype(BF16)

    def z_send(i, carry):
        own = is_self(from_z(i))

        @pl.when(own)
        def _():
            z_rx[my_t] = z_tx[i]

        @pl.when(jnp.logical_not(own))
        def _():
            rcopy(
                z_tx.at[i], z_rx.at[my_t], z_ss.at[i], z_rs.at[my_t], dev(x, y, from_z(i), zhalf)
            ).start()

        return carry

    lax.fori_loop(0, nt, z_send, 0)

    def z_recv(i, carry):
        @pl.when(jnp.logical_not(is_self(to_z(i))))
        def _():
            rcopy(z_tx.at[i], z_rx.at[i], z_ss.at[0], z_rs.at[i], sib_dev).wait_recv()

        return carry

    lax.fori_loop(0, nt, z_recv, 0)

    z_sum = jnp.sum(z_rx[...].astype(F32), axis=0)
    for core in range(CORES):
        x_tx[core, 0:lanes] = z_sum[core * lanes : (core + 1) * lanes]
        x_tx[core, lanes:] = z_sum[(2 + core) * lanes : (3 + core) * lanes]
    x_rx[x, c] = x_tx[c]

    def x_send(o, carry):
        dx, core = lax.div(o, CORES), lax.rem(c + lax.rem(o, CORES), CORES)
        rcopy(
            x_tx.at[core], x_rx.at[x, c], x_ss.at[o], x_rs.at[x, c], dev(lax.rem(x + dx, nx), y, z, core)
        ).start()
        return carry

    lax.fori_loop(1, CORES * nx, x_send, 0)

    def x_recv(o, carry):
        dx, core = lax.div(o, CORES), lax.rem(c + lax.rem(o, CORES), CORES)
        slot = lax.rem(x - dx + nx, nx)
        rcopy(x_tx.at[0], x_rx.at[slot, core], x_ss.at[0], x_rs.at[slot, core], sib_dev).wait_recv()
        return carry

    lax.fori_loop(1, CORES * nx, x_recv, 0)
    for core in range(CORES):
        done = jnp.sum(x_rx[:, core], axis=0)
        gk_ref[:, core * HD : (core + 1) * HD] = done[:lanes] * scale
        gv_ref[:, core * HD : (core + 1) * HD] = done[lanes:]

    def near_done(i, carry):
        @pl.when(jnp.logical_not(is_self(to_z(i))))
        def _():
            near_copy(i).wait_send()

        @pl.when(jnp.logical_not(is_self(from_z(i))))
        def _():
            rcopy(z_tx.at[i], z_rx.at[0], z_ss.at[i], z_rs.at[0], sib_dev).wait_send()

        return carry

    lax.fori_loop(0, nt, near_done, 0)

    def plane_done(o, carry):
        rcopy(kv.at[c, me], kv.at[c, me], gat_ss.at[o], gat_rs.at[0], sib_dev).wait_send()
        for part in range(2):
            rcopy(
                pl_tx.at[part, 0], pl_rx.at[part, 0], pl_ss.at[part, o], pl_rs.at[part, 0], sib_dev
            ).wait_send()
        return carry

    lax.fori_loop(1, plane, plane_done, 0)

    def x_done(o, carry):
        rcopy(x_tx.at[0], x_rx.at[0, 0], x_ss.at[o], x_rs.at[0, 0], sib_dev).wait_send()
        return carry

    lax.fori_loop(1, CORES * nx, x_done, 0)
    gq_out.wait()


def make(mesh, ny):
    nx = mesh.shape["resp"]
    zl = mesh.shape["ep"] // ny
    zh = mesh.shape["kv"] // CORES
    geo = (nx, ny, zl, zh)
    plane = nx * ny
    nt = zl * zh // KVH // nx

    def body(lengths, queries, grad_out, prompt_keys, prompt_values):
        rows = queries.shape[1]
        width = queries.shape[2] // mesh.shape["kv"]
        lanes = prompt_keys.shape[0]
        blk = nt * CORES * lanes
        span = CORES * plane * blk
        dma = pltpu.SemaphoreType.DMA
        vmem = pl.BlockSpec(memory_space=pltpu.VMEM)
        hbm = pl.BlockSpec(memory_space=pltpu.HBM)
        return pl.pallas_call(
            functools.partial(kernel, geo),
            out_shape=(
                jax.ShapeDtypeStruct((1, rows, width), F32),
                jax.ShapeDtypeStruct(prompt_keys.shape, F32),
                jax.ShapeDtypeStruct(prompt_values.shape, F32),
            ),
            in_specs=[pl.BlockSpec(memory_space=pltpu.SMEM), hbm, hbm, vmem, vmem],
            out_specs=(hbm, vmem, vmem),
            scratch_shapes=[
                pltpu.VMEM((rows, width), BF16),
                pltpu.VMEM((rows, width), BF16),
                pltpu.VMEM((2 * lanes, HD), F32),
                pltpu.VMEM((2 * lanes, HD), F32),
                pltpu.VMEM((4 * lanes, HD), F32),
                pltpu.VMEM((4 * lanes, HD), BF16),
                pltpu.VMEM((nt, 4 * lanes, HD), BF16),
                pltpu.VMEM((CORES, plane, 2, blk, HD), BF16),
                pltpu.VMEM((span, rows * width // HD), BF16),
                pltpu.VMEM((span, rows * width // HD), BF16),
                pltpu.VMEM((2, CORES, span // 2, HD), F32),
                pltpu.VMEM((2, span // 2, HD), F32),
                pltpu.VMEM((2, plane, blk, HD), BF16),
                pltpu.VMEM((2, plane, blk, HD), BF16),
                pltpu.VMEM((nt, 4 * lanes, HD), BF16),
                pltpu.VMEM((nt, 4 * lanes, HD), BF16),
                pltpu.VMEM((CORES, 2 * lanes, HD), F32),
                pltpu.VMEM((nx, CORES, 2 * lanes, HD), F32),
                pltpu.VMEM((rows, width), F32),
                dma((2,)),
                dma,
                dma,
                dma,
                dma((nt,)),
                dma((nt,)),
                dma((plane,)),
                dma((plane,)),
                dma,
                dma,
                dma((2,)),
                dma((2,)),
                dma((2, plane)),
                dma((2, plane)),
                dma((nt,)),
                dma((nt,)),
                dma((CORES * nx,)),
                dma((nx, CORES)),
            ],
            compiler_params=pltpu.CompilerParams(
                collective_id=0, has_side_effects=True, vmem_limit_bytes=40 * 1024 * 1024
            ),
        )(lengths, queries, grad_out, prompt_keys, prompt_values)

    return jax.shard_map(
        body,
        mesh=mesh,
        in_specs=(
            P(),
            P("resp", "ep", None),
            P("resp", "ep", None),
            P(("ep", "kv"), None),
            P(("ep", "kv"), None),
        ),
        out_specs=(P("resp", "ep", "kv"), P(("ep", "kv"), None), P(("ep", "kv"), None)),
        check_vma=False,
    )


def solution(mesh):
    return make(mesh, NY)
```

time: 907 us -> 83 us (0.09)
  the two profiles are of different devices: /device:TPU:32 before, /device:TPU:1 now
where the time goes in v1:
time: 83 us; the launch traced here: 82.7 us
  Pallas kernels  75.7 us (91%)
  local copies, waits for them, and re-layouts  6.35 us (8%)
    pallas_call x1, Pallas kernels, body(): pl.pallas_call(functools.partial(kernel, geo), out_shape=(jax.ShapeDtypeS...  75.7 us
    unnamed x13, local copies, waits for them, and re-layouts  6.35 us

profile of v1, /device:TPU:1, one launch (start us, length us, event | category | flops | bytes accessed | tf_op | source)
XLA Modules:
  0.0 82.7 jit_solution(15488097892706346322)
XLA Ops:
  0.6 0.0 copy-start
  0.6 1.2 %copy-done = bf16[1,128,4096]{2,1,0:T(8,128)(2,1)S(1)} copy-done((bf16[1,128,4096]{2,1,0:T(8,128)(2,1)S(1)}, bf16[1,128,4096]{2,1,0:T(8,128)(2,1)}, u32[]{:S(2)}) %copy-start) | copy-done | bytes 1048600
  1.9 0.0 copy-start.1
  1.9 1.2 %copy-done.1 = bf16[1,128,4096]{2,1,0:T(8,128)(2,1)S(1)} copy-done((bf16[1,128,4096]{2,1,0:T(8,128)(2,1)S(1)}, bf16[1,128,4096]{2,1,0:T(8,128)(2,1)}, u32[]{:S(2)}) %copy-start.1) | copy-done | bytes 1048600
  3.1 0.0 copy-start.2
  3.1 0.7 copy-done.2
  3.8 0.0 copy-start.3
  3.8 0.7 copy-done.3
  4.4 0.0 copy-start.4
  4.4 0.7 copy-done.4
  5.1 75.7 %shard_map.76 = (f32[1,128,512]{2,1,0:T(8,128)S(1)}, f32[4,256]{1,0:T(4,128)S(1)}, f32[4,256]{1,0:T(4,128)S(1)}) custom-call(s32[4]{0:T(128)S(1)} %copy-done.4, bf16[1,128,4096]{2,1,0:T(8,128)(2,1)S(1)} %copy-done, bf16[1,128,4096]{2,1,0:T(8,128)(2,1)S(1)} %copy-done.1, bf16[4,256]{1,0:T(4,128)(2,1)S(1)} %copy-done.2, bf16[4,256]{1,0:T(4,128)(2,1)S(1)} %copy-done.3), custom_call_target="tpu_custom_call" | custom-call | tf_op jit(solution)/shard_map/pallas_call | solution.py:401
  80.8 0.7 copy.11
  81.5 0.6 copy.12
  82.1 0.6 copy.13
Async XLA Ops:
  0.6 1.2 %copy-start = (bf16[1,128,4096]{2,1,0:T(8,128)(2,1)S(1)}, bf16[1,128,4096]{2,1,0:T(8,128)(2,1)}, u32[]{:S(2)}) copy-start(bf16[1,128,4096]{2,1,0:T(8,128)(2,1)} %q_hbm.1) | copy-start | bytes 3145732
  1.9 1.2 %copy-start.1 = (bf16[1,128,4096]{2,1,0:T(8,128)(2,1)S(1)}, bf16[1,128,4096]{2,1,0:T(8,128)(2,1)}, u32[]{:S(2)}) copy-start(bf16[1,128,4096]{2,1,0:T(8,128)(2,1)} %g_hbm.1) | copy-start | bytes 3145732
  3.1 0.7 copy-start.2
  3.8 0.7 copy-start.3
  4.4 0.7 copy-start.4

commit v2 on v0

v2 whole, which is shorter than its diff:
```python
import functools
import math

import jax
import jax.numpy as jnp
from jax import lax
from jax.experimental import pallas as pl
from jax.experimental.pallas import tpu as pltpu
from jax.sharding import PartitionSpec as P

HD = 128
KVH = 2
CORES = 2
NY = 4
MESH = pl.DeviceIdType.MESH
BF16 = jnp.bfloat16
F32 = jnp.float32


def kernel(
    geo,
    len_hbm,
    q_hbm,
    g_hbm,
    k_hbm,
    v_hbm,
    gq_hbm,
    gk_hbm,
    gv_hbm,
    len_s,
    k_v,
    v_v,
    q_v,
    g_v,
    q_s,
    g_s,
    pack_f,
    pack,
    near,
    rows_f,
    kb,
    vb,
    p_t,
    ds_t,
    acc,
    acc_rx,
    one_tx,
    one_rx,
    two_tx,
    two_rx,
    z_tx,
    z_rx,
    x_tx,
    x_rx,
    gq_v,
    gk_v,
    gv_v,
    in_sem,
    out_sem,
    near_ss,
    near_rs,
    kb_ss,
    kb_rs,
    vb_ss,
    vb_rs,
    sib_ss,
    sib_rs,
    acc_ss,
    acc_rs,
    one_ss,
    one_rs,
    two_ss,
    two_rs,
    z_ss,
    z_rs,
    x_ss,
    x_rs,
):
    nx, ny, zl, zh = geo
    nz = zl * zh
    half = nz // KVH
    far = nz // 4
    rows = q_v.shape[0]
    width = q_v.shape[1]
    heads = width // HD
    lanes = k_v.shape[0]
    blk = kb.shape[3]
    span = CORES * nx * ny * blk
    scale = 1.0 / math.sqrt(HD)

    x = lax.axis_index("resp")
    ep = lax.axis_index("ep")
    kvi = lax.axis_index("kv")
    y, z_lo = lax.div(ep, zl), lax.rem(ep, zl)
    z_hi, c = lax.div(kvi, CORES), lax.rem(kvi, CORES)
    z = z_hi * zl + z_lo

    def at_z(offset):
        zz = lax.rem(z + offset + nz, nz)
        return (x, y * zl + lax.rem(zz, zl), lax.div(zz, zl) * CORES + c)

    def at_x(offset):
        return (lax.rem(x + offset + nx, nx), ep, kvi)

    def at_y(offset):
        return (x, lax.rem(y + offset + ny, ny) * zl + z_lo, kvi)

    sib = (x, ep, z_hi * CORES + 1 - c)

    first = jnp.where(x == 0, nx, x)
    second = first + nx
    direct = [first, second, -first, -second]
    relayed = [first + far, second + far, -first - far, jnp.where(x == 0, 0, -second - far)]
    offsets = direct + relayed
    count = len(offsets)

    barrier = pltpu.get_barrier_semaphore()
    peers = [at_z(o) for o in (-far, far, -second, second, -first, first)]
    peers += [at_y(o) for o in range(1, ny)] + [at_x(o) for o in range(1, nx)] + [sib]
    for peer in peers:
        pl.semaphore_signal(barrier, inc=1, device_id=peer, device_id_type=MESH)

    copies = [
        pltpu.make_async_copy(k_hbm, k_v, in_sem.at[0]),
        pltpu.make_async_copy(v_hbm, v_v, in_sem.at[1]),
        pltpu.make_async_copy(len_hbm, len_s, in_sem.at[2]),
    ]
    own = pl.ds(pl.multiple_of(kvi * width, width), width)
    copies.append(pltpu.make_async_copy(q_hbm.at[0, :, own], q_v, in_sem.at[3]))
    copies.append(pltpu.make_async_copy(g_hbm.at[0, :, own], g_v, in_sem.at[4]))
    for copy in copies:
        copy.start()

    sent = []

    def send(src, dst, ss, rs, device):
        copy = pltpu.make_async_remote_copy(
            src_ref=src, dst_ref=dst, send_sem=ss, recv_sem=rs, device_id=device, device_id_type=MESH
        )
        copy.start()
        sent.append(copy)
        return copy

    copies[0].wait()
    copies[1].wait()
    for h in range(KVH):
        for part, ref in enumerate((k_v, v_v)):
            at = (2 * h + part) * lanes
            pack_f[at : at + lanes] = ref[:, h * HD : (h + 1) * HD].astype(F32)
    pack[...] = pack_f[...].astype(BF16)
    pl.semaphore_wait(barrier, len(peers))

    z_in = [send(pack, near.at[i], near_ss.at[i], near_rs.at[i], at_z(-direct[i])) for i in (1, 3, 0, 2)]
    z_in[0].wait_recv()
    z_in[2].wait_recv()
    fwd_up = send(near.at[0:2], near.at[4:6], near_ss.at[4], near_rs.at[4], at_z(-far))
    z_in[1].wait_recv()
    z_in[3].wait_recv()
    fwd_down = send(near.at[2:4], near.at[6:8], near_ss.at[5], near_rs.at[5], at_z(far))

    for copy in copies[2:]:
        copy.wait()
    valid = ep * rows + lax.broadcasted_iota(jnp.int32, (rows, HD), 0) < len_s[x]
    for h in range(heads):
        cols = slice(h * HD, (h + 1) * HD)
        at = slice(h * rows, (h + 1) * rows)
        q_s[at] = q_v[:, cols]
        g_s[at] = jnp.where(valid, g_v[:, cols], jnp.zeros((), BF16))

    fwd_up.wait_recv()
    fwd_down.wait_recv()

    mine = lax.div(z, half)
    for i in range(count):
        packet = near[i].astype(F32)
        if i == count - 1:
            packet = jnp.where(x == 0, pack_f[...], packet)
        packet = jnp.where(mine == 0, packet[: 2 * lanes], packet[2 * lanes :])
        rows_f[0, i * lanes : (i + 1) * lanes] = packet[:lanes]
        rows_f[1, i * lanes : (i + 1) * lanes] = packet[lanes:]
    kb[0, 0, 0] = rows_f[0].astype(BF16)
    vb[0, 0, 0] = rows_f[1].astype(BF16)

    k_one = [send(kb.at[0, 0, 0], kb.at[0, 0, o], kb_ss.at[0, o], kb_rs.at[0, o], at_x(o)) for o in range(1, nx)]
    v_one = [send(vb.at[0, 0, 0], vb.at[0, o, 0], vb_ss.at[0, o], vb_rs.at[0, o], at_y(o)) for o in range(1, ny)]
    for copy in k_one:
        copy.wait_recv()
    k_two = [send(kb.at[0, 0], kb.at[0, o], kb_ss.at[1, o], kb_rs.at[1, o], at_y(o)) for o in range(1, ny)]
    for copy in v_one:
        copy.wait_recv()
    v_two = [
        send(vb.at[0, :, 0], vb.at[0, :, o], vb_ss.at[1, o], vb_rs.at[1, o], at_x(o)) for o in range(1, nx)
    ]
    shared = [
        send(kb.at[0, 0], kb.at[1, 0], sib_ss.at[0], sib_rs.at[0], sib),
        send(vb.at[0, :, 0], vb.at[1, :, 0], sib_ss.at[1], sib_rs.at[1], sib),
    ]
    for copy in k_two:
        copy.wait_recv()
    shared.append(send(kb.at[0, 1:ny], kb.at[1, 1:ny], sib_ss.at[2], sib_rs.at[2], sib))
    for copy in v_two:
        copy.wait_recv()
    shared.append(send(vb.at[0, :, 1:nx], vb.at[1, :, 1:nx], sib_ss.at[3], sib_rs.at[3], sib))
    for copy in shared:
        copy.wait_recv()

    keys = kb[...].reshape(span, HD)
    values = vb[...].reshape(span, HD)
    factor = scale * math.log2(math.e)
    for h in range(heads):
        at = slice(h * rows, (h + 1) * rows)
        s = lax.dot_general(keys, q_s[at], (((1,), (1,)), ((), ())), preferred_element_type=F32)
        top = jnp.max(s, axis=0, keepdims=True)
        e = jnp.exp2((s - top) * factor)
        prob = e * (1.0 / jnp.sum(e, axis=0, keepdims=True))
        p_t[:, at] = prob.astype(BF16)
        dp = lax.dot_general(values, g_s[at], (((1,), (1,)), ((), ())), preferred_element_type=F32)
        delta = jnp.sum(prob * dp, axis=0, keepdims=True)
        ds_t[:, at] = (prob * (dp - delta)).astype(BF16)

    def partial(part, weights, operand):
        total = jnp.dot(weights[...], operand[...], preferred_element_type=F32)
        acc[part] = total.reshape(CORES, ny, nx, blk, HD)
        return send(acc.at[part, 1], acc_rx.at[part], acc_ss.at[part], acc_rs.at[part], sib)

    v_acc = partial(1, p_t, g_s)
    k_acc = partial(0, ds_t, q_s)

    v_acc.wait_recv()
    v_all = acc[1, 0] + acc_rx[1]
    for o in range(1, nx):
        one_tx[1, o] = v_all[:, o].astype(BF16)
    v_one = [
        send(one_tx.at[1, o], one_rx.at[1, o], one_ss.at[1, o], one_rs.at[1, o], at_x(-o)) for o in range(1, nx)
    ]
    acc[1, 0, :, 0] = v_all[:, 0]
    k_acc.wait_recv()
    k_all = acc[0, 0] + acc_rx[0]
    for o in range(1, ny):
        one_tx[0, o] = k_all[o].astype(BF16)
    k_one = [
        send(one_tx.at[0, o], one_rx.at[0, o], one_ss.at[0, o], one_rs.at[0, o], at_y(-o)) for o in range(1, ny)
    ]
    acc[0, 0, 0] = k_all[0]

    for copy in v_one:
        copy.wait_recv()
    v_half = acc[1, 0, :, 0]
    for o in range(1, nx):
        v_half += one_rx[1, o].astype(F32)
    two_tx[1] = v_half
    v_two = [
        send(two_tx.at[1, o], two_rx.at[1, o], two_ss.at[1, o], two_rs.at[1, o], at_y(-o)) for o in range(1, ny)
    ]
    for copy in k_one:
        copy.wait_recv()
    k_half = acc[0, 0, 0]
    for o in range(1, ny):
        k_half += one_rx[0, o].astype(F32)
    two_tx[0] = k_half
    k_two = [
        send(two_tx.at[0, o], two_rx.at[0, o], two_ss.at[0, o], two_rs.at[0, o], at_x(-o)) for o in range(1, nx)
    ]
    for copy in v_two:
        copy.wait_recv()
    for copy in k_two:
        copy.wait_recv()
    for part, size in ((0, nx), (1, ny)):
        total = two_tx[part, 0]
        for o in range(1, size):
            total += two_rx[part, o]
        rows_f[part] = total
    for i in range(count):
        for part in range(2):
            z_tx[i, part * lanes : (part + 1) * lanes] = rows_f[part, i * lanes : (i + 1) * lanes]

    def z_copy(i):
        return pltpu.make_async_remote_copy(
            src_ref=z_tx.at[i],
            dst_ref=z_rx.at[i],
            send_sem=z_ss.at[i],
            recv_sem=z_rs.at[i],
            device_id=at_z(offsets[i]),
            device_id_type=MESH,
        )

    for i in (5, 4, 6, 1, 3, 0, 2):
        z_copy(i).start()

    @pl.when(x != 0)
    def _():
        z_copy(count - 1).start()

    @pl.when(x == 0)
    def _():
        z_rx[count - 1] = z_tx[count - 1]

    gq_t = jnp.dot(keys.T, ds_t[...], preferred_element_type=F32) * scale
    for h in range(heads):
        gq_v[:, h * HD : (h + 1) * HD] = gq_t[:, h * rows : (h + 1) * rows].T
    gq_out = pltpu.make_async_copy(gq_v, gq_hbm.at[0], out_sem.at[0])
    gq_out.start()

    for i in range(count - 1):
        z_copy(i).wait_recv()

    @pl.when(x != 0)
    def _():
        z_copy(count - 1).wait_recv()

    for h in range(KVH):
        total = jnp.zeros((2 * lanes, HD), F32)
        for i in range(count):
            source = lax.rem(z - offsets[i] + nz, nz)
            total += jnp.where(lax.div(source, half) == h, z_rx[i], 0.0)
        x_tx[h] = total
    last = [send(x_tx, x_rx.at[o], x_ss.at[o], x_rs.at[o], at_x(o)) for o in range(1, nx)]
    for copy in last:
        copy.wait_recv()
    for h in range(KVH):
        total = x_tx[h]
        for o in range(1, nx):
            total += x_rx[o, h]
        gk_v[:, h * HD : (h + 1) * HD] = total[:lanes] * scale
        gv_v[:, h * HD : (h + 1) * HD] = total[lanes:]
    gk_out = pltpu.make_async_copy(gk_v, gk_hbm, out_sem.at[1])
    gv_out = pltpu.make_async_copy(gv_v, gv_hbm, out_sem.at[2])
    gk_out.start()
    gv_out.start()

    for copy in sent:
        copy.wait_send()
    for i in range(count - 1):
        z_copy(i).wait_send()

    @pl.when(x != 0)
    def _():
        z_copy(count - 1).wait_send()

    gq_out.wait()
    gk_out.wait()
    gv_out.wait()


def hand_over(gq, gk, gv, gq_out, gk_out, gv_out):
    gq_out[...] = gq[...]
    gk_out[...] = gk[...]
    gv_out[...] = gv[...]


def make(mesh, ny):
    nx = mesh.shape["resp"]
    zl = mesh.shape["ep"] // ny
    zh = mesh.shape["kv"] // CORES
    geo = (nx, ny, zl, zh)
    count = zl * zh // nx

    def body(lengths, queries, grad_out, prompt_keys, prompt_values):
        rows = queries.shape[1]
        width = queries.shape[2] // mesh.shape["kv"]
        lanes = prompt_keys.shape[0]
        blk = count * lanes
        span = CORES * nx * ny * blk
        stacked = rows * width // HD
        side = max(nx, ny)
        dma = pltpu.SemaphoreType.DMA
        hbm = pl.BlockSpec(memory_space=pltpu.HBM)
        out_shape = (
            jax.ShapeDtypeStruct((1, rows, width), F32),
            jax.ShapeDtypeStruct(prompt_keys.shape, F32),
            jax.ShapeDtypeStruct(prompt_values.shape, F32),
        )
        grads = pl.pallas_call(
            functools.partial(kernel, geo),
            out_shape=out_shape,
            in_specs=[hbm] * 5,
            out_specs=(hbm, hbm, hbm),
            scratch_shapes=[
                pltpu.SMEM(lengths.shape, jnp.int32),
                pltpu.VMEM(prompt_keys.shape, BF16),
                pltpu.VMEM(prompt_values.shape, BF16),
                pltpu.VMEM((rows, width), BF16),
                pltpu.VMEM((rows, width), BF16),
                pltpu.VMEM((stacked, HD), BF16),
                pltpu.VMEM((stacked, HD), BF16),
                pltpu.VMEM((4 * lanes, HD), F32),
                pltpu.VMEM((4 * lanes, HD), BF16),
                pltpu.VMEM((count, 4 * lanes, HD), BF16),
                pltpu.VMEM((2, blk, HD), F32),
                pltpu.VMEM((CORES, ny, nx, blk, HD), BF16),
                pltpu.VMEM((CORES, ny, nx, blk, HD), BF16),
                pltpu.VMEM((span, stacked), BF16),
                pltpu.VMEM((span, stacked), BF16),
                pltpu.VMEM((2, CORES, ny, nx, blk, HD), F32),
                pltpu.VMEM((2, ny, nx, blk, HD), F32),
                pltpu.VMEM((2, side, side, blk, HD), BF16),
                pltpu.VMEM((2, side, side, blk, HD), BF16),
                pltpu.VMEM((2, side, blk, HD), F32),
                pltpu.VMEM((2, side, blk, HD), F32),
                pltpu.VMEM((count, 2 * lanes, HD), F32),
                pltpu.VMEM((count, 2 * lanes, HD), F32),
                pltpu.VMEM((KVH, 2 * lanes, HD), F32),
                pltpu.VMEM((nx, KVH, 2 * lanes, HD), F32),
                pltpu.VMEM((rows, width), F32),
                pltpu.VMEM(prompt_keys.shape, F32),
                pltpu.VMEM(prompt_values.shape, F32),
                dma((5,)),
                dma((3,)),
                dma((6,)),
                dma((6,)),
                dma((2, side)),
                dma((2, side)),
                dma((2, side)),
                dma((2, side)),
                dma((4,)),
                dma((4,)),
                dma((2,)),
                dma((2,)),
                dma((2, side)),
                dma((2, side)),
                dma((2, side)),
                dma((2, side)),
                dma((count,)),
                dma((count,)),
                dma((nx,)),
                dma((nx,)),
            ],
            compiler_params=pltpu.CompilerParams(
                collective_id=0, has_side_effects=True, vmem_limit_bytes=60 * 1024 * 1024
            ),
        )(lengths, queries, grad_out, prompt_keys, prompt_values)
        return pl.pallas_call(hand_over, out_shape=out_shape)(*grads)

    return jax.shard_map(
        body,
        mesh=mesh,
        in_specs=(
            P(),
            P("resp", "ep", None),
            P("resp", "ep", None),
            P(("ep", "kv"), None),
            P(("ep", "kv"), None),
        ),
        out_specs=(P("resp", "ep", "kv"), P(("ep", "kv"), None), P(("ep", "kv"), None)),
        check_vma=False,
    )


def solution(mesh):
    return make(mesh, NY)
```

time: 907 us -> 76.1 us (0.08)
  the two profiles are of different devices: /device:TPU:32 before, /device:TPU:4 now
where the time goes in v2:
time: 76.1 us; the launch traced here: 75.9 us
  Pallas kernels  75.3 us (99%)
    pallas_call x1, Pallas kernels, body(): pl.pallas_call(functools.partial(kernel, geo), out_shape=out_shape, in_sp...  73.6 us
    pallas_call x1, Pallas kernels, body(): return pl.pallas_call(hand_over, out_shape=out_shape)(*grads)  1.68 us

profile of v2, /device:TPU:4, one launch (start us, length us, event | category | flops | bytes accessed | tf_op | source)
XLA Modules:
  0.0 75.9 jit_solution(7534916189427934898)
XLA Ops:
  0.6 73.6 %shard_map.76 = (f32[1,128,512]{2,1,0:T(8,128)}, f32[4,256]{1,0:T(4,128)}, f32[4,256]{1,0:T(4,128)}) custom-call(s32[4]{0:T(128)} %len_hbm.1, bf16[1,128,4096]{2,1,0:T(8,128)(2,1)} %q_hbm.1, bf16[1,128,4096]{2,1,0:T(8,128)(2,1)} %g_hbm.1, bf16[4,256]{1,0:T(4,128)(2,1)} %k_hbm.1, bf16[4,256]{1,0:T(4,128)(2,1)} %v_hbm.1), custom_call_target="tpu_custom_call" | custom-call | tf_op jit(solution)/shard_map/pallas_call | solution.py:373
  74.3 1.7 %shard_map.77 = (f32[1,128,512]{2,1,0:T(8,128)}, f32[4,256]{1,0:T(4,128)}, f32[4,256]{1,0:T(4,128)}) custom-call(f32[1,128,512]{2,1,0:T(8,128)} %get-tuple-element.6.gq, f32[4,256]{1,0:T(4,128)} %get-tuple-element.7.gk, f32[4,256]{1,0:T(4,128)} %get-tuple-element.8.gv), custom_call_target="tpu_custom_call" | custom-call | tf_op jit(solution)/shard_map/pallas_call | solution.py:432

commit v3 on v2

--- a/solution.py
+++ b/solution.py
@@ -38,12 +38,14 @@
     pack,
     near,
     rows_f,
-    kb,
-    vb,
+    kv,
+    s_f,
+    dp_f,
     p_t,
     ds_t,
     acc,
     acc_rx,
+    kept,
     one_tx,
     one_rx,
     two_tx,
@@ -59,10 +61,8 @@
     out_sem,
     near_ss,
     near_rs,
-    kb_ss,
-    kb_rs,
-    vb_ss,
-    vb_rs,
+    kv_ss,
+    kv_rs,
     sib_ss,
     sib_rs,
     acc_ss,
@@ -84,8 +84,9 @@
     width = q_v.shape[1]
     heads = width // HD
     lanes = k_v.shape[0]
-    blk = kb.shape[3]
-    span = CORES * nx * ny * blk
+    part_rows = kv.shape[5]
+    span = CORES * 2 * nx * ny * part_rows
+    mid = span // 2
     scale = 1.0 / math.sqrt(HD)
 
     x = lax.axis_index("resp")
@@ -105,7 +106,13 @@
     def at_y(offset):
         return (x, lax.rem(y + offset + ny, ny) * zl + z_lo, kvi)
 
+    def in_plane(ox, oy):
+        return (lax.rem(x + ox, nx), lax.rem(y + oy, ny) * zl + z_lo, kvi)
+
     sib = (x, ep, z_hi * CORES + 1 - c)
+
+    plane = [(ox, oy) for ox in range(nx) for oy in range(ny) if ox or oy]
+    plane.sort(key=lambda o: -min(o[0], nx - o[0]) - min(o[1], ny - o[1]))
 
     first = jnp.where(x == 0, nx, x)
     second = first + nx
@@ -116,7 +123,7 @@
 
     barrier = pltpu.get_barrier_semaphore()
     peers = [at_z(o) for o in (-far, far, -second, second, -first, first)]
-    peers += [at_y(o) for o in range(1, ny)] + [at_x(o) for o in range(1, nx)] + [sib]
+    peers += [in_plane(*o) for o in plane] + [sib]
     for peer in peers:
         pl.semaphore_signal(barrier, inc=1, device_id=peer, device_id_type=MESH)
 
@@ -151,12 +158,6 @@
     pl.semaphore_wait(barrier, len(peers))
 
     z_in = [send(pack, near.at[i], near_ss.at[i], near_rs.at[i], at_z(-direct[i])) for i in (1, 3, 0, 2)]
-    z_in[0].wait_recv()
-    z_in[2].wait_recv()
-    fwd_up = send(near.at[0:2], near.at[4:6], near_ss.at[4], near_rs.at[4], at_z(-far))
-    z_in[1].wait_recv()
-    z_in[3].wait_recv()
-    fwd_down = send(near.at[2:4], near.at[6:8], near_ss.at[5], near_rs.at[5], at_z(far))
 
     for copy in copies[2:]:
         copy.wait()
@@ -167,97 +168,118 @@
         q_s[at] = q_v[:, cols]
         g_s[at] = jnp.where(valid, g_v[:, cols], jnp.zeros((), BF16))
 
+    z_in[0].wait_recv()
+    z_in[2].wait_recv()
+    fwd_up = send(near.at[0:2], near.at[4:6], near_ss.at[4], near_rs.at[4], at_z(-far))
+    z_in[1].wait_recv()
+    z_in[3].wait_recv()
+    fwd_down = send(near.at[2:4], near.at[6:8], near_ss.at[5], near_rs.at[5], at_z(far))
+
+    mine = lax.div(z, half)
+    per = count // 2
+
+    def plane_gather(part):
+        for i in range(part * per, (part + 1) * per):
+            packet = near[i].astype(F32)
+            if i == count - 1:
+                packet = jnp.where(x == 0, pack_f[...], packet)
+            packet = jnp.where(mine == 0, packet[: 2 * lanes], packet[2 * lanes :])
+            rows_f[0, i * lanes : (i + 1) * lanes] = packet[:lanes]
+            rows_f[1, i * lanes : (i + 1) * lanes] = packet[lanes:]
+        span_rows = slice(part * part_rows, (part + 1) * part_rows)
+        for side in range(2):
+            kv[part, 0, 0, 0, side] = rows_f[side, span_rows].astype(BF16)
+        return [
+            send(
+                kv.at[part, 0, 0, 0],
+                kv.at[part, 0, oy, ox],
+                kv_ss.at[part, oy, ox],
+                kv_rs.at[part, oy, ox],
+                in_plane(ox, oy),
+            )
+            for ox, oy in plane
+        ]
+
+    def share(part, arriving):
+        for copy in reversed(arriving):
+            copy.wait_recv()
+        return send(kv.at[part, 0], kv.at[part, 1], sib_ss.at[part], sib_rs.at[part], sib)
+
+    def half_of(part, side):
+        return kv[part, :, :, :, side].reshape(mid, HD)
+
+    def against(table, operand):
+        return lax.dot_general(table, operand, (((1,), (1,)), ((), ())), preferred_element_type=F32)
+
+    half_one = plane_gather(0)
     fwd_up.wait_recv()
     fwd_down.wait_recv()
-
-    mine = lax.div(z, half)
-    for i in range(count):
-        packet = near[i].astype(F32)
-        if i == count - 1:
-            packet = jnp.where(x == 0, pack_f[...], packet)
-        packet = jnp.where(mine == 0, packet[: 2 * lanes], packet[2 * lanes :])
-        rows_f[0, i * lanes : (i + 1) * lanes] = packet[:lanes]
-        rows_f[1, i * lanes : (i + 1) * lanes] = packet[lanes:]
-    kb[0, 0, 0] = rows_f[0].astype(BF16)
-    vb[0, 0, 0] = rows_f[1].astype(BF16)
-
-    k_one = [send(kb.at[0, 0, 0], kb.at[0, 0, o], kb_ss.at[0, o], kb_rs.at[0, o], at_x(o)) for o in range(1, nx)]
-    v_one = [send(vb.at[0, 0, 0], vb.at[0, o, 0], vb_ss.at[0, o], vb_rs.at[0, o], at_y(o)) for o in range(1, ny)]
-    for copy in k_one:
-        copy.wait_recv()
-    k_two = [send(kb.at[0, 0], kb.at[0, o], kb_ss.at[1, o], kb_rs.at[1, o], at_y(o)) for o in range(1, ny)]
-    for copy in v_one:
-        copy.wait_recv()
-    v_two = [
-        send(vb.at[0, :, 0], vb.at[0, :, o], vb_ss.at[1, o], vb_rs.at[1, o], at_x(o)) for o in range(1, nx)
-    ]
-    shared = [
-        send(kb.at[0, 0], kb.at[1, 0], sib_ss.at[0], sib_rs.at[0], sib),
-        send(vb.at[0, :, 0], vb.at[1, :, 0], sib_ss.at[1], sib_rs.at[1], sib),
-    ]
-    for copy in k_two:
-        copy.wait_recv()
-    shared.append(send(kb.at[0, 1:ny], kb.at[1, 1:ny], sib_ss.at[2], sib_rs.at[2], sib))
-    for copy in v_two:
-        copy.wait_recv()
-    shared.append(send(vb.at[0, :, 1:nx], vb.at[1, :, 1:nx], sib_ss.at[3], sib_rs.at[3], sib))
-    for copy in shared:
-        copy.wait_recv()
-
-    keys = kb[...].reshape(span, HD)
-    values = vb[...].reshape(span, HD)
+    half_two = plane_gather(1)
+    share_one = share(0, half_one)
+    share_one.wait_recv()
+    s_f[...] = against(half_of(0, 0), q_s[...])
+    dp_f[...] = against(half_of(0, 1), g_s[...])
+    share(1, half_two).wait_recv()
+
+    keys_two = half_of(1, 0)
+    values_two = half_of(1, 1)
     factor = scale * math.log2(math.e)
     for h in range(heads):
         at = slice(h * rows, (h + 1) * rows)
-        s = lax.dot_general(keys, q_s[at], (((1,), (1,)), ((), ())), preferred_element_type=F32)
-        top = jnp.max(s, axis=0, keepdims=True)
-        e = jnp.exp2((s - top) * factor)
-        prob = e * (1.0 / jnp.sum(e, axis=0, keepdims=True))
-        p_t[:, at] = prob.astype(BF16)
-        dp = lax.dot_general(values, g_s[at], (((1,), (1,)), ((), ())), preferred_element_type=F32)
-        delta = jnp.sum(prob * dp, axis=0, keepdims=True)
-        ds_t[:, at] = (prob * (dp - delta)).astype(BF16)
-
-    def partial(part, weights, operand):
+        s = [s_f[:, at], against(keys_two, q_s[at])]
+        top = jnp.maximum(*[jnp.max(v, axis=0, keepdims=True) for v in s])
+        e = [jnp.exp2((v - top) * factor) for v in s]
+        inverse = 1.0 / sum(jnp.sum(v, axis=0, keepdims=True) for v in e)
+        prob = [v * inverse for v in e]
+        dp = [dp_f[:, at], against(values_two, g_s[at])]
+        delta = sum(jnp.sum(p * d, axis=0, keepdims=True) for p, d in zip(prob, dp))
+        for i in range(2):
+            block = slice(i * mid, (i + 1) * mid)
+            p_t[block, at] = prob[i].astype(BF16)
+            ds_t[block, at] = (prob[i] * (dp[i] - delta)).astype(BF16)
+
+    def partial(side, weights, operand):
         total = jnp.dot(weights[...], operand[...], preferred_element_type=F32)
-        acc[part] = total.reshape(CORES, ny, nx, blk, HD)
-        return send(acc.at[part, 1], acc_rx.at[part], acc_ss.at[part], acc_rs.at[part], sib)
+        acc[side] = total.reshape(2, CORES, ny, nx, part_rows, HD)
+        return send(acc.at[side, :, 1], acc_rx.at[side], acc_ss.at[side], acc_rs.at[side], sib)
 
     v_acc = partial(1, p_t, g_s)
     k_acc = partial(0, ds_t, q_s)
 
     v_acc.wait_recv()
-    v_all = acc[1, 0] + acc_rx[1]
+    v_all = acc[1, :, 0] + acc_rx[1]
     for o in range(1, nx):
-        one_tx[1, o] = v_all[:, o].astype(BF16)
+        one_tx[1, o] = v_all[:, :, o].astype(BF16)
     v_one = [
         send(one_tx.at[1, o], one_rx.at[1, o], one_ss.at[1, o], one_rs.at[1, o], at_x(-o)) for o in range(1, nx)
     ]
-    acc[1, 0, :, 0] = v_all[:, 0]
+    kept[1] = v_all[:, :, 0]
     k_acc.wait_recv()
-    k_all = acc[0, 0] + acc_rx[0]
+    k_all = acc[0, :, 0] + acc_rx[0]
     for o in range(1, ny):
-        one_tx[0, o] = k_all[o].astype(BF16)
+        one_tx[0, o] = k_all[:, o].astype(BF16)
     k_one = [
         send(one_tx.at[0, o], one_rx.at[0, o], one_ss.at[0, o], one_rs.at[0, o], at_y(-o)) for o in range(1, ny)
     ]
-    acc[0, 0, 0] = k_all[0]
+    kept[0] = k_all[:, 0]
 
     for copy in v_one:
         copy.wait_recv()
-    v_half = acc[1, 0, :, 0]
+    v_half = kept[1]
     for o in range(1, nx):
         v_half += one_rx[1, o].astype(F32)
-    two_tx[1] = v_half
+    for o in range(ny):
+        two_tx[1, o] = v_half[:, o]
     v_two = [
         send(two_tx.at[1, o], two_rx.at[1, o], two_ss.at[1, o], two_rs.at[1, o], at_y(-o)) for o in range(1, ny)
     ]
     for copy in k_one:
         copy.wait_recv()
-    k_half = acc[0, 0, 0]
+    k_half = kept[0]
     for o in range(1, ny):
         k_half += one_rx[0, o].astype(F32)
-    two_tx[0] = k_half
+    for o in range(nx):
+        two_tx[0, o] = k_half[:, o]
     k_two = [
         send(two_tx.at[0, o], two_rx.at[0, o], two_ss.at[0, o], two_rs.at[0, o], at_x(-o)) for o in range(1, nx)
     ]
@@ -269,7 +291,7 @@
         total = two_tx[part, 0]
         for o in range(1, size):
             total += two_rx[part, o]
-        rows_f[part] = total
+        rows_f[part] = total.reshape(2 * part_rows, HD)
     for i in range(count):
         for part in range(2):
             z_tx[i, part * lanes : (part + 1) * lanes] = rows_f[part, i * lanes : (i + 1) * lanes]
@@ -295,11 +317,14 @@
     def _():
         z_rx[count - 1] = z_tx[count - 1]
 
+    keys = kv[:, :, :, :, 0].reshape(span, HD)
     gq_t = jnp.dot(keys.T, ds_t[...], preferred_element_type=F32) * scale
     for h in range(heads):
         gq_v[:, h * HD : (h + 1) * HD] = gq_t[:, h * rows : (h + 1) * rows].T
     gq_out = pltpu.make_async_copy(gq_v, gq_hbm.at[0], out_sem.at[0])
     gq_out.start()
+    while sent:
+        sent.pop().wait_send()
 
     for i in range(count - 1):
         z_copy(i).wait_recv()
@@ -315,6 +340,13 @@
             total += jnp.where(lax.div(source, half) == h, z_rx[i], 0.0)
         x_tx[h] = total
     last = [send(x_tx, x_rx.at[o], x_ss.at[o], x_rs.at[o], at_x(o)) for o in range(1, nx)]
+    for i in range(count - 1):
+        z_copy(i).wait_send()
+
+    @pl.when(x != 0)
+    def _():
+        z_copy(count - 1).wait_send()
+
     for copy in last:
         copy.wait_recv()
     for h in range(KVH):
@@ -328,15 +360,8 @@
     gk_out.start()
     gv_out.start()
 
-    for copy in sent:
-        copy.wait_send()
-    for i in range(count - 1):
-        z_copy(i).wait_send()
-
-    @pl.when(x != 0)
-    def _():
-        z_copy(count - 1).wait_send()
-
+    while sent:
+        sent.pop().wait_send()
     gq_out.wait()
     gk_out.wait()
     gv_out.wait()
@@ -359,8 +384,8 @@
         rows = queries.shape[1]
         width = queries.shape[2] // mesh.shape["kv"]
         lanes = prompt_keys.shape[0]
-        blk = count * lanes
-        span = CORES * nx * ny * blk
+        part_rows = count * lanes // 2
+        span = CORES * 2 * nx * ny * part_rows
         stacked = rows * width // HD
         side = max(nx, ny)
         dma = pltpu.SemaphoreType.DMA
@@ -386,17 +411,19 @@
                 pltpu.VMEM((4 * lanes, HD), F32),
                 pltpu.VMEM((4 * lanes, HD), BF16),
                 pltpu.VMEM((count, 4 * lanes, HD), BF16),
-                pltpu.VMEM((2, blk, HD), F32),
-                pltpu.VMEM((CORES, ny, nx, blk, HD), BF16),
-                pltpu.VMEM((CORES, ny, nx, blk, HD), BF16),
+                pltpu.VMEM((2, 2 * part_rows, HD), F32),
+                pltpu.VMEM((2, CORES, ny, nx, 2, part_rows, HD), BF16),
+                pltpu.VMEM((span // 2, stacked), F32),
+                pltpu.VMEM((span // 2, stacked), F32),
                 pltpu.VMEM((span, stacked), BF16),
                 pltpu.VMEM((span, stacked), BF16),
-                pltpu.VMEM((2, CORES, ny, nx, blk, HD), F32),
-                pltpu.VMEM((2, ny, nx, blk, HD), F32),
-                pltpu.VMEM((2, side, side, blk, HD), BF16),
-                pltpu.VMEM((2, side, side, blk, HD), BF16),
-                pltpu.VMEM((2, side, blk, HD), F32),
-                pltpu.VMEM((2, side, blk, HD), F32),
+                pltpu.VMEM((2, 2, CORES, ny, nx, part_rows, HD), F32),
+                pltpu.VMEM((2, 2, ny, nx, part_rows, HD), F32),
+                pltpu.VMEM((2, 2, side, part_rows, HD), F32),
+                pltpu.VMEM((2, side, 2, side, part_rows, HD), BF16),
+                pltpu.VMEM((2, side, 2, side, part_rows, HD), BF16),
+                pltpu.VMEM((2, side, 2, part_rows, HD), F32),
+                pltpu.VMEM((2, side, 2, part_rows, HD), F32),
                 pltpu.VMEM((count, 2 * lanes, HD), F32),
                 pltpu.VMEM((count, 2 * lanes, HD), F32),
                 pltpu.VMEM((KVH, 2 * lanes, HD), F32),
@@ -408,12 +435,10 @@
                 dma((3,)),
                 dma((6,)),
                 dma((6,)),
-                dma((2, side)),
-                dma((2, side)),
-                dma((2, side)),
-                dma((2, side)),
-                dma((4,)),
-                dma((4,)),
+                dma((2, ny, nx)),
+                dma((2, ny, nx)),
+                dma((2,)),
+                dma((2,)),
                 dma((2,)),
                 dma((2,)),
                 dma((2, side)),

time: 76.1 us -> 73 us (0.959)
  the two profiles are of different devices: /device:TPU:4 before, /device:TPU:2 now
where the time goes in v3:
time: 73 us; the launch traced here: 72.9 us
  Pallas kernels  72.2 us (99%)
    pallas_call x1, Pallas kernels, body(): pl.pallas_call(functools.partial(kernel, geo), out_shape=out_shape, in_sp...  70.5 us
    pallas_call x1, Pallas kernels, body(): return pl.pallas_call(hand_over, out_shape=out_shape)(*grads)  1.68 us

profile of v3, /device:TPU:2, one launch (start us, length us, event | category | flops | bytes accessed | tf_op | source)
XLA Modules:
  0.0 72.9 jit_solution(10896453792527403962)
XLA Ops:
  0.6 70.5 %shard_map.76 = (f32[1,128,512]{2,1,0:T(8,128)}, f32[4,256]{1,0:T(4,128)}, f32[4,256]{1,0:T(4,128)}) custom-call(s32[4]{0:T(128)} %len_hbm.1, bf16[1,128,4096]{2,1,0:T(8,128)(2,1)} %q_hbm.1, bf16[1,128,4096]{2,1,0:T(8,128)(2,1)} %g_hbm.1, bf16[4,256]{1,0:T(4,128)(2,1)} %k_hbm.1, bf16[4,256]{1,0:T(4,128)(2,1)} %v_hbm.1), custom_call_target="tpu_custom_call" | custom-call | tf_op jit(solution)/shard_map/pallas_call | solution.py:398
  71.2 1.7 %shard_map.77 = (f32[1,128,512]{2,1,0:T(8,128)}, f32[4,256]{1,0:T(4,128)}, f32[4,256]{1,0:T(4,128)}) custom-call(f32[1,128,512]{2,1,0:T(8,128)} %get-tuple-element.6.gq, f32[4,256]{1,0:T(4,128)} %get-tuple-element.7.gk, f32[4,256]{1,0:T(4,128)} %get-tuple-element.8.gv), custom_call_target="tpu_custom_call" | custom-call | tf_op jit(solution)/shard_map/pallas_call | solution.py:457

commit v4 on v3

--- a/solution.py
+++ b/solution.py
@@ -48,8 +48,6 @@
     kept,
     one_tx,
     one_rx,
-    two_tx,
-    two_rx,
     z_tx,
     z_rx,
     x_tx,
@@ -69,8 +67,6 @@
     acc_rs,
     one_ss,
     one_rs,
-    two_ss,
-    two_rs,
     z_ss,
     z_rs,
     x_ss,
@@ -103,11 +99,8 @@
     def at_x(offset):
         return (lax.rem(x + offset + nx, nx), ep, kvi)
 
-    def at_y(offset):
-        return (x, lax.rem(y + offset + ny, ny) * zl + z_lo, kvi)
-
     def in_plane(ox, oy):
-        return (lax.rem(x + ox, nx), lax.rem(y + oy, ny) * zl + z_lo, kvi)
+        return (lax.rem(x + ox + nx, nx), lax.rem(y + oy + ny, ny) * zl + z_lo, kvi)
 
     sib = (x, ep, z_hi * CORES + 1 - c)
 
@@ -246,52 +239,34 @@
     v_acc = partial(1, p_t, g_s)
     k_acc = partial(0, ds_t, q_s)
 
-    v_acc.wait_recv()
-    v_all = acc[1, :, 0] + acc_rx[1]
-    for o in range(1, nx):
-        one_tx[1, o] = v_all[:, :, o].astype(BF16)
-    v_one = [
-        send(one_tx.at[1, o], one_rx.at[1, o], one_ss.at[1, o], one_rs.at[1, o], at_x(-o)) for o in range(1, nx)
-    ]
-    kept[1] = v_all[:, :, 0]
-    k_acc.wait_recv()
-    k_all = acc[0, :, 0] + acc_rx[0]
-    for o in range(1, ny):
-        one_tx[0, o] = k_all[:, o].astype(BF16)
-    k_one = [
-        send(one_tx.at[0, o], one_rx.at[0, o], one_ss.at[0, o], one_rs.at[0, o], at_y(-o)) for o in range(1, ny)
-    ]
-    kept[0] = k_all[:, 0]
-
-    for copy in v_one:
+    def scatter(side, copy):
         copy.wait_recv()
-    v_half = kept[1]
-    for o in range(1, nx):
-        v_half += one_rx[1, o].astype(F32)
-    for o in range(ny):
-        two_tx[1, o] = v_half[:, o]
-    v_two = [
-        send(two_tx.at[1, o], two_rx.at[1, o], two_ss.at[1, o], two_rs.at[1, o], at_y(-o)) for o in range(1, ny)
-    ]
-    for copy in k_one:
-        copy.wait_recv()
-    k_half = kept[0]
-    for o in range(1, ny):
-        k_half += one_rx[0, o].astype(F32)
-    for o in range(nx):
-        two_tx[0, o] = k_half[:, o]
-    k_two = [
-        send(two_tx.at[0, o], two_rx.at[0, o], two_ss.at[0, o], two_rs.at[0, o], at_x(-o)) for o in range(1, nx)
-    ]
-    for copy in v_two:
-        copy.wait_recv()
-    for copy in k_two:
-        copy.wait_recv()
-    for part, size in ((0, nx), (1, ny)):
-        total = two_tx[part, 0]
-        for o in range(1, size):
-            total += two_rx[part, o]
-        rows_f[part] = total.reshape(2 * part_rows, HD)
+        both = acc[side, :, 0] + acc_rx[side]
+        kept[side] = both[:, 0, 0]
+        for ox, oy in plane:
+            one_tx[side, oy, ox] = both[:, oy, ox].astype(BF16)
+        return [
+            send(
+                one_tx.at[side, oy, ox],
+                one_rx.at[side, oy, ox],
+                one_ss.at[side, oy, ox],
+                one_rs.at[side, oy, ox],
+                in_plane(-ox, -oy),
+            )
+            for ox, oy in plane
+        ]
+
+    def collect(side, arriving):
+        total = kept[side]
+        for copy, (ox, oy) in reversed(list(zip(arriving, plane))):
+            copy.wait_recv()
+            total += one_rx[side, oy, ox].astype(F32)
+        rows_f[side] = total.reshape(2 * part_rows, HD)
+
+    v_one = scatter(1, v_acc)
+    k_one = scatter(0, k_acc)
+    collect(1, v_one)
+    collect(0, k_one)
     for i in range(count):
         for part in range(2):
             z_tx[i, part * lanes : (part + 1) * lanes] = rows_f[part, i * lanes : (i + 1) * lanes]
@@ -387,7 +362,6 @@
         part_rows = count * lanes // 2
         span = CORES * 2 * nx * ny * part_rows
         stacked = rows * width // HD
-        side = max(nx, ny)
         dma = pltpu.SemaphoreType.DMA
         hbm = pl.BlockSpec(memory_space=pltpu.HBM)
         out_shape = (
@@ -419,11 +393,9 @@
                 pltpu.VMEM((span, stacked), BF16),
                 pltpu.VMEM((2, 2, CORES, ny, nx, part_rows, HD), F32),
                 pltpu.VMEM((2, 2, ny, nx, part_rows, HD), F32),
-                pltpu.VMEM((2, 2, side, part_rows, HD), F32),
-                pltpu.VMEM((2, side, 2, side, part_rows, HD), BF16),
-                pltpu.VMEM((2, side, 2, side, part_rows, HD), BF16),
-                pltpu.VMEM((2, side, 2, part_rows, HD), F32),
-                pltpu.VMEM((2, side, 2, part_rows, HD), F32),
+                pltpu.VMEM((2, 2, part_rows, HD), F32),
+                pltpu.VMEM((2, ny, nx, 2, part_rows, HD), BF16),
+                pltpu.VMEM((2, ny, nx, 2, part_rows, HD), BF16),
                 pltpu.VMEM((count, 2 * lanes, HD), F32),
                 pltpu.VMEM((count, 2 * lanes, HD), F32),
                 pltpu.VMEM((KVH, 2 * lanes, HD), F32),
@@ -441,10 +413,8 @@
                 dma((2,)),
                 dma((2,)),
                 dma((2,)),
-                dma((2, side)),
-                dma((2, side)),
-                dma((2, side)),
-                dma((2, side)),
+                dma((2, ny, nx)),
+                dma((2, ny, nx)),
                 dma((count,)),
                 dma((count,)),
                 dma((nx,)),

time: 73 us -> 71 us (0.973)
  Pallas kernels: 72.2 us -> 70.2 us
    pallas_call x1, Pallas kernels: 70.5 us -> 68.5 us  [body(): pl.pallas_call(functools.partial(kernel, geo), out_shape=out_shape, in_sp...]
where the time goes in v4:
time: 71 us; the launch traced here: 70.8 us
  Pallas kernels  70.2 us (99%)
    pallas_call x1, Pallas kernels, body(): pl.pallas_call(functools.partial(kernel, geo), out_shape=out_shape, in_sp...  68.5 us
    pallas_call x1, Pallas kernels, body(): return pl.pallas_call(hand_over, out_shape=out_shape)(*grads)  1.68 us

profile of v4, /device:TPU:2, one launch (start us, length us, event | category | flops | bytes accessed | tf_op | source)
XLA Modules:
  0.0 70.8 jit_solution(12703995209968733000)
XLA Ops:
  0.6 68.5 %shard_map.76 = (f32[1,128,512]{2,1,0:T(8,128)}, f32[4,256]{1,0:T(4,128)}, f32[4,256]{1,0:T(4,128)}) custom-call(s32[4]{0:T(128)} %len_hbm.1, bf16[1,128,4096]{2,1,0:T(8,128)(2,1)} %q_hbm.1, bf16[1,128,4096]{2,1,0:T(8,128)(2,1)} %g_hbm.1, bf16[4,256]{1,0:T(4,128)(2,1)} %k_hbm.1, bf16[4,256]{1,0:T(4,128)(2,1)} %v_hbm.1), custom_call_target="tpu_custom_call" | custom-call | tf_op jit(solution)/shard_map/pallas_call | solution.py:372
  69.1 1.7 %shard_map.77 = (f32[1,128,512]{2,1,0:T(8,128)}, f32[4,256]{1,0:T(4,128)}, f32[4,256]{1,0:T(4,128)}) custom-call(f32[1,128,512]{2,1,0:T(8,128)} %get-tuple-element.6.gq, f32[4,256]{1,0:T(4,128)} %get-tuple-element.7.gk, f32[4,256]{1,0:T(4,128)} %get-tuple-element.8.gv), custom_call_target="tpu_custom_call" | custom-call | tf_op jit(solution)/shard_map/pallas_call | solution.py:427

commit v5 on v4

--- a/solution.py
+++ b/solution.py
@@ -39,19 +39,22 @@
     near,
     rows_f,
     kv,
-    s_f,
+    e_f,
     dp_f,
+    st_half,
+    st_tx,
+    st_rx,
     p_t,
     ds_t,
     acc,
-    acc_rx,
-    kept,
     one_tx,
     one_rx,
     z_tx,
     z_rx,
     x_tx,
     x_rx,
+    gq_p,
+    gq_rx,
     gq_v,
     gk_v,
     gv_v,
@@ -61,10 +64,10 @@
     near_rs,
     kv_ss,
     kv_rs,
-    sib_ss,
-    sib_rs,
-    acc_ss,
-    acc_rs,
+    st_ss,
+    st_rs,
+    gq_ss,
+    gq_rs,
     one_ss,
     one_rs,
     z_ss,
@@ -80,8 +83,8 @@
     width = q_v.shape[1]
     heads = width // HD
     lanes = k_v.shape[0]
-    part_rows = kv.shape[5]
-    span = CORES * 2 * nx * ny * part_rows
+    part_rows = kv.shape[4]
+    span = 2 * nx * ny * part_rows
     mid = span // 2
     scale = 1.0 / math.sqrt(HD)
 
@@ -125,7 +128,7 @@
         pltpu.make_async_copy(v_hbm, v_v, in_sem.at[1]),
         pltpu.make_async_copy(len_hbm, len_s, in_sem.at[2]),
     ]
-    own = pl.ds(pl.multiple_of(kvi * width, width), width)
+    own = pl.ds(pl.multiple_of(z_hi * width, width), width)
     copies.append(pltpu.make_async_copy(q_hbm.at[0, :, own], q_v, in_sem.at[3]))
     copies.append(pltpu.make_async_copy(g_hbm.at[0, :, own], g_v, in_sem.at[4]))
     for copy in copies:
@@ -181,11 +184,11 @@
             rows_f[1, i * lanes : (i + 1) * lanes] = packet[lanes:]
         span_rows = slice(part * part_rows, (part + 1) * part_rows)
         for side in range(2):
-            kv[part, 0, 0, 0, side] = rows_f[side, span_rows].astype(BF16)
+            kv[part, 0, 0, side] = rows_f[side, span_rows].astype(BF16)
         return [
             send(
-                kv.at[part, 0, 0, 0],
-                kv.at[part, 0, oy, ox],
+                kv.at[part, 0, 0],
+                kv.at[part, oy, ox],
                 kv_ss.at[part, oy, ox],
                 kv_rs.at[part, oy, ox],
                 in_plane(ox, oy),
@@ -193,13 +196,8 @@
             for ox, oy in plane
         ]
 
-    def share(part, arriving):
-        for copy in reversed(arriving):
-            copy.wait_recv()
-        return send(kv.at[part, 0], kv.at[part, 1], sib_ss.at[part], sib_rs.at[part], sib)
-
     def half_of(part, side):
-        return kv[part, :, :, :, side].reshape(mid, HD)
+        return kv[part, :, :, side].reshape(mid, HD)
 
     def against(table, operand):
         return lax.dot_general(table, operand, (((1,), (1,)), ((), ())), preferred_element_type=F32)
@@ -208,65 +206,62 @@
     fwd_up.wait_recv()
     fwd_down.wait_recv()
     half_two = plane_gather(1)
-    share_one = share(0, half_one)
-    share_one.wait_recv()
-    s_f[...] = against(half_of(0, 0), q_s[...])
-    dp_f[...] = against(half_of(0, 1), g_s[...])
-    share(1, half_two).wait_recv()
-
-    keys_two = half_of(1, 0)
-    values_two = half_of(1, 1)
     factor = scale * math.log2(math.e)
-    for h in range(heads):
-        at = slice(h * rows, (h + 1) * rows)
-        s = [s_f[:, at], against(keys_two, q_s[at])]
-        top = jnp.maximum(*[jnp.max(v, axis=0, keepdims=True) for v in s])
-        e = [jnp.exp2((v - top) * factor) for v in s]
-        inverse = 1.0 / sum(jnp.sum(v, axis=0, keepdims=True) for v in e)
-        prob = [v * inverse for v in e]
-        dp = [dp_f[:, at], against(values_two, g_s[at])]
-        delta = sum(jnp.sum(p * d, axis=0, keepdims=True) for p, d in zip(prob, dp))
-        for i in range(2):
-            block = slice(i * mid, (i + 1) * mid)
-            p_t[block, at] = prob[i].astype(BF16)
-            ds_t[block, at] = (prob[i] * (dp[i] - delta)).astype(BF16)
-
-    def partial(side, weights, operand):
-        total = jnp.dot(weights[...], operand[...], preferred_element_type=F32)
-        acc[side] = total.reshape(2, CORES, ny, nx, part_rows, HD)
-        return send(acc.at[side, :, 1], acc_rx.at[side], acc_ss.at[side], acc_rs.at[side], sib)
-
-    v_acc = partial(1, p_t, g_s)
-    k_acc = partial(0, ds_t, q_s)
-
-    def scatter(side, copy):
+
+    def first_pass(part, arriving):
+        for copy in reversed(arriving):
+            copy.wait_recv()
+        block = slice(part * mid, (part + 1) * mid)
+        keys, values = half_of(part, 0), half_of(part, 1)
+        for h in range(heads):
+            at = slice(h * rows, (h + 1) * rows)
+            s = against(keys, q_s[at])
+            dp = against(values, g_s[at])
+            top = jnp.max(s, axis=0, keepdims=True)
+            e = jnp.exp2((s - top) * factor)
+            e_f[block, at] = e
+            dp_f[block, at] = dp
+            st_half[part, 0, h : h + 1, :rows] = top
+            st_half[part, 1, h : h + 1, :rows] = jnp.sum(e, axis=0, keepdims=True)
+            st_half[part, 2, h : h + 1, :rows] = jnp.sum(e * dp, axis=0, keepdims=True)
+
+    first_pass(0, half_one)
+    first_pass(1, half_two)
+
+    def joined(stats):
+        joint = jnp.maximum(stats[0][0], stats[1][0])
+        weights = [jnp.exp2((stat[0] - joint) * factor) for stat in stats]
+        return [joint] + [sum(stat[k] * w for stat, w in zip(stats, weights)) for k in (1, 2)]
+
+    st_tx[0], st_tx[1], st_tx[2] = joined([st_half[0], st_half[1]])
+    send(st_tx, st_rx, st_ss, st_rs, sib).wait_recv()
+    joint, total, inner = joined([st_tx[...], st_rx[...]])
+    inverse = 1.0 / total
+    delta = inner * inverse
+    for part in range(2):
+        block = slice(part * mid, (part + 1) * mid)
+        weight = jnp.exp2((st_half[part, 0] - joint) * factor) * inverse
+        for h in range(heads):
+            at = slice(h * rows, (h + 1) * rows)
+            prob = e_f[block, at] * weight[h : h + 1, :rows]
+            p_t[block, at] = prob.astype(BF16)
+            ds_t[block, at] = (prob * (dp_f[block, at] - delta[h : h + 1, :rows])).astype(BF16)
+
+    for side, weights, operand in ((0, ds_t, q_s), (1, p_t, g_s)):
+        part_sum = jnp.dot(weights[...], operand[...], preferred_element_type=F32)
+        part_sum = part_sum.reshape(2, ny, nx, part_rows, HD)
+        acc[side] = part_sum[:, 0, 0]
+        for ox, oy in plane:
+            one_tx[oy, ox, side] = part_sum[:, oy, ox].astype(BF16)
+    arriving = [
+        send(one_tx.at[oy, ox], one_rx.at[oy, ox], one_ss.at[oy, ox], one_rs.at[oy, ox], in_plane(-ox, -oy))
+        for ox, oy in plane
+    ]
+    plane_sum = acc[...]
+    for copy, (ox, oy) in reversed(list(zip(arriving, plane))):
         copy.wait_recv()
-        both = acc[side, :, 0] + acc_rx[side]
-        kept[side] = both[:, 0, 0]
-        for ox, oy in plane:
-            one_tx[side, oy, ox] = both[:, oy, ox].astype(BF16)
-        return [
-            send(
-                one_tx.at[side, oy, ox],
-                one_rx.at[side, oy, ox],
-                one_ss.at[side, oy, ox],
-                one_rs.at[side, oy, ox],
-                in_plane(-ox, -oy),
-            )
-            for ox, oy in plane
-        ]
-
-    def collect(side, arriving):
-        total = kept[side]
-        for copy, (ox, oy) in reversed(list(zip(arriving, plane))):
-            copy.wait_recv()
-            total += one_rx[side, oy, ox].astype(F32)
-        rows_f[side] = total.reshape(2 * part_rows, HD)
-
-    v_one = scatter(1, v_acc)
-    k_one = scatter(0, k_acc)
-    collect(1, v_one)
-    collect(0, k_one)
+        plane_sum += one_rx[oy, ox].astype(F32)
+    rows_f[...] = plane_sum.reshape(2, 2 * part_rows, HD)
     for i in range(count):
         for part in range(2):
             z_tx[i, part * lanes : (part + 1) * lanes] = rows_f[part, i * lanes : (i + 1) * lanes]
@@ -292,9 +287,14 @@
     def _():
         z_rx[count - 1] = z_tx[count - 1]
 
-    keys = kv[:, :, :, :, 0].reshape(span, HD)
-    gq_t = jnp.dot(keys.T, ds_t[...], preferred_element_type=F32) * scale
-    for h in range(heads):
+    keys_t = kv[:, :, :, 0].reshape(span, HD).T
+    own_cols = heads // CORES * rows
+    for core in range(CORES):
+        block = slice(core * own_cols, (core + 1) * own_cols)
+        gq_p[core] = jnp.dot(keys_t, ds_t[:, block], preferred_element_type=F32)
+    send(gq_p.at[1 - c], gq_rx, gq_ss, gq_rs, sib).wait_recv()
+    gq_t = (gq_p[c] + gq_rx[...]) * scale
+    for h in range(heads // CORES):
         gq_v[:, h * HD : (h + 1) * HD] = gq_t[:, h * rows : (h + 1) * rows].T
     gq_out = pltpu.make_async_copy(gq_v, gq_hbm.at[0], out_sem.at[0])
     gq_out.start()
@@ -360,8 +360,10 @@
         width = queries.shape[2] // mesh.shape["kv"]
         lanes = prompt_keys.shape[0]
         part_rows = count * lanes // 2
-        span = CORES * 2 * nx * ny * part_rows
-        stacked = rows * width // HD
+        span = 2 * nx * ny * part_rows
+        both = CORES * width
+        heads = both // HD
+        stacked = rows * heads
         dma = pltpu.SemaphoreType.DMA
         hbm = pl.BlockSpec(memory_space=pltpu.HBM)
         out_shape = (
@@ -378,28 +380,31 @@
                 pltpu.SMEM(lengths.shape, jnp.int32),
                 pltpu.VMEM(prompt_keys.shape, BF16),
                 pltpu.VMEM(prompt_values.shape, BF16),
-                pltpu.VMEM((rows, width), BF16),
-                pltpu.VMEM((rows, width), BF16),
+                pltpu.VMEM((rows, both), BF16),
+                pltpu.VMEM((rows, both), BF16),
                 pltpu.VMEM((stacked, HD), BF16),
                 pltpu.VMEM((stacked, HD), BF16),
                 pltpu.VMEM((4 * lanes, HD), F32),
                 pltpu.VMEM((4 * lanes, HD), BF16),
                 pltpu.VMEM((count, 4 * lanes, HD), BF16),
                 pltpu.VMEM((2, 2 * part_rows, HD), F32),
-                pltpu.VMEM((2, CORES, ny, nx, 2, part_rows, HD), BF16),
-                pltpu.VMEM((span // 2, stacked), F32),
-                pltpu.VMEM((span // 2, stacked), F32),
+                pltpu.VMEM((2, ny, nx, 2, part_rows, HD), BF16),
+                pltpu.VMEM((span, stacked), F32),
+                pltpu.VMEM((span, stacked), F32),
+                pltpu.VMEM((2, 3, heads, HD), F32),
+                pltpu.VMEM((3, heads, HD), F32),
+                pltpu.VMEM((3, heads, HD), F32),
                 pltpu.VMEM((span, stacked), BF16),
                 pltpu.VMEM((span, stacked), BF16),
-                pltpu.VMEM((2, 2, CORES, ny, nx, part_rows, HD), F32),
-                pltpu.VMEM((2, 2, ny, nx, part_rows, HD), F32),
                 pltpu.VMEM((2, 2, part_rows, HD), F32),
-                pltpu.VMEM((2, ny, nx, 2, part_rows, HD), BF16),
-                pltpu.VMEM((2, ny, nx, 2, part_rows, HD), BF16),
+                pltpu.VMEM((ny, nx, 2, 2, part_rows, HD), BF16),
+                pltpu.VMEM((ny, nx, 2, 2, part_rows, HD), BF16),
                 pltpu.VMEM((count, 2 * lanes, HD), F32),
                 pltpu.VMEM((count, 2 * lanes, HD), F32),
                 pltpu.VMEM((KVH, 2 * lanes, HD), F32),
                 pltpu.VMEM((nx, KVH, 2 * lanes, HD), F32),
+                pltpu.VMEM((CORES, HD, stacked // CORES), F32),
+                pltpu.VMEM((HD, stacked // CORES), F32),
                 pltpu.VMEM((rows, width), F32),
                 pltpu.VMEM(prompt_keys.shape, F32),
                 pltpu.VMEM(prompt_values.shape, F32),
@@ -409,12 +414,12 @@
                 dma((6,)),
                 dma((2, ny, nx)),
                 dma((2, ny, nx)),
-                dma((2,)),
-                dma((2,)),
-                dma((2,)),
-                dma((2,)),
-                dma((2, ny, nx)),
-                dma((2, ny, nx)),
+                dma,
+                dma,
+                dma,
+                dma,
+                dma((ny, nx)),
+                dma((ny, nx)),
                 dma((count,)),
                 dma((count,)),
                 dma((nx,)),

time: 71 us -> 68.8 us (0.969)
  the two profiles are of different devices: /device:TPU:2 before, /device:TPU:1 now
where the time goes in v5:
time: 68.8 us; the launch traced here: 68.6 us
  Pallas kernels  68 us (99%)
    pallas_call x1, Pallas kernels, body(): pl.pallas_call(functools.partial(kernel, geo), out_shape=out_shape, in_sp...  66.3 us
    pallas_call x1, Pallas kernels, body(): return pl.pallas_call(hand_over, out_shape=out_shape)(*grads)  1.68 us

profile of v5, /device:TPU:1, one launch (start us, length us, event | category | flops | bytes accessed | tf_op | source)
XLA Modules:
  0.0 68.6 jit_solution(2360987343235433698)
XLA Ops:
  0.6 66.3 %shard_map.76 = (f32[1,128,512]{2,1,0:T(8,128)}, f32[4,256]{1,0:T(4,128)}, f32[4,256]{1,0:T(4,128)}) custom-call(s32[4]{0:T(128)} %len_hbm.1, bf16[1,128,4096]{2,1,0:T(8,128)(2,1)} %q_hbm.1, bf16[1,128,4096]{2,1,0:T(8,128)(2,1)} %g_hbm.1, bf16[4,256]{1,0:T(4,128)(2,1)} %k_hbm.1, bf16[4,256]{1,0:T(4,128)(2,1)} %v_hbm.1), custom_call_target="tpu_custom_call" | custom-call | tf_op jit(solution)/shard_map/pallas_call | solution.py:374
  66.9 1.7 %shard_map.77 = (f32[1,128,512]{2,1,0:T(8,128)}, f32[4,256]{1,0:T(4,128)}, f32[4,256]{1,0:T(4,128)}) custom-call(f32[1,128,512]{2,1,0:T(8,128)} %get-tuple-element.6.gq, f32[4,256]{1,0:T(4,128)} %get-tuple-element.7.gk, f32[4,256]{1,0:T(4,128)} %get-tuple-element.8.gv), custom_call_target="tpu_custom_call" | custom-call | tf_op jit(solution)/shard_map/pallas_call | solution.py:432

commit v6 on v5

--- a/solution.py
+++ b/solution.py
@@ -24,9 +24,9 @@
     g_hbm,
     k_hbm,
     v_hbm,
-    gq_hbm,
-    gk_hbm,
-    gv_hbm,
+    gq_ref,
+    gk_ref,
+    gv_ref,
     len_s,
     k_v,
     v_v,
@@ -55,11 +55,7 @@
     x_rx,
     gq_p,
     gq_rx,
-    gq_v,
-    gk_v,
-    gv_v,
     in_sem,
-    out_sem,
     near_ss,
     near_rs,
     kv_ss,
@@ -295,9 +291,7 @@
     send(gq_p.at[1 - c], gq_rx, gq_ss, gq_rs, sib).wait_recv()
     gq_t = (gq_p[c] + gq_rx[...]) * scale
     for h in range(heads // CORES):
-        gq_v[:, h * HD : (h + 1) * HD] = gq_t[:, h * rows : (h + 1) * rows].T
-    gq_out = pltpu.make_async_copy(gq_v, gq_hbm.at[0], out_sem.at[0])
-    gq_out.start()
+        gq_ref[0, :, h * HD : (h + 1) * HD] = gq_t[:, h * rows : (h + 1) * rows].T
     while sent:
         sent.pop().wait_send()
 
@@ -328,24 +322,11 @@
         total = x_tx[h]
         for o in range(1, nx):
             total += x_rx[o, h]
-        gk_v[:, h * HD : (h + 1) * HD] = total[:lanes] * scale
-        gv_v[:, h * HD : (h + 1) * HD] = total[lanes:]
-    gk_out = pltpu.make_async_copy(gk_v, gk_hbm, out_sem.at[1])
-    gv_out = pltpu.make_async_copy(gv_v, gv_hbm, out_sem.at[2])
-    gk_out.start()
-    gv_out.start()
+        gk_ref[:, h * HD : (h + 1) * HD] = total[:lanes] * scale
+        gv_ref[:, h * HD : (h + 1) * HD] = total[lanes:]
 
     while sent:
         sent.pop().wait_send()
-    gq_out.wait()
-    gk_out.wait()
-    gv_out.wait()
-
-
-def hand_over(gq, gk, gv, gq_out, gk_out, gv_out):
-    gq_out[...] = gq[...]
-    gk_out[...] = gk[...]
-    gv_out[...] = gv[...]
 
 
 def make(mesh, ny):
@@ -365,17 +346,20 @@
         heads = both // HD
         stacked = rows * heads
         dma = pltpu.SemaphoreType.DMA
+        vmem = pl.BlockSpec(memory_space=pltpu.VMEM)
         hbm = pl.BlockSpec(memory_space=pltpu.HBM)
         out_shape = (
             jax.ShapeDtypeStruct((1, rows, width), F32),
             jax.ShapeDtypeStruct(prompt_keys.shape, F32),
             jax.ShapeDtypeStruct(prompt_values.shape, F32),
         )
-        grads = pl.pallas_call(
+        operands = (lengths, queries, grad_out, prompt_keys, prompt_values)
+        operands = [pltpu.with_memory_space_constraint(a, pltpu.HBM) for a in operands]
+        return pl.pallas_call(
             functools.partial(kernel, geo),
             out_shape=out_shape,
             in_specs=[hbm] * 5,
-            out_specs=(hbm, hbm, hbm),
+            out_specs=(vmem, vmem, vmem),
             scratch_shapes=[
                 pltpu.SMEM(lengths.shape, jnp.int32),
                 pltpu.VMEM(prompt_keys.shape, BF16),
@@ -405,11 +389,7 @@
                 pltpu.VMEM((nx, KVH, 2 * lanes, HD), F32),
                 pltpu.VMEM((CORES, HD, stacked // CORES), F32),
                 pltpu.VMEM((HD, stacked // CORES), F32),
-                pltpu.VMEM((rows, width), F32),
-                pltpu.VMEM(prompt_keys.shape, F32),
-                pltpu.VMEM(prompt_values.shape, F32),
                 dma((5,)),
-                dma((3,)),
                 dma((6,)),
                 dma((6,)),
                 dma((2, ny, nx)),
@@ -426,10 +406,9 @@
                 dma((nx,)),
             ],
             compiler_params=pltpu.CompilerParams(
-                collective_id=0, has_side_effects=True, vmem_limit_bytes=60 * 1024 * 1024
+                collective_id=0, has_side_effects=True, vmem_limit_bytes=40 * 1024 * 1024
             ),
-        )(lengths, queries, grad_out, prompt_keys, prompt_values)
-        return pl.pallas_call(hand_over, out_shape=out_shape)(*grads)
+        )(*operands)
 
     return jax.shard_map(
         body,

time: 68.8 us -> 68.3 us (level)
  Pallas kernels: 68 us -> 65.7 us
  local copies, waits for them, and re-layouts: 0 us -> 1.89 us
    unnamed x0 -> x3, local copies, waits for them, and re-layouts: none -> 1.89 us
    pallas_call x1 -> x0, Pallas kernels: 1.68 us -> none  [body(): return pl.pallas_call(hand_over, out_shape=out_shape)(*grads)]
where the time goes in v6:
time: 68.3 us; the launch traced here: 68.2 us
  Pallas kernels  65.7 us (96%)
  local copies, waits for them, and re-layouts  1.89 us (3%)
    pallas_call x1, Pallas kernels, body(): pl.pallas_call(functools.partial(kernel, geo), out_shape=out_shape, in_sp...  65.7 us
    unnamed x3, local copies, waits for them, and re-layouts  1.89 us

profile of v6, /device:TPU:1, one launch (start us, length us, event | category | flops | bytes accessed | tf_op | source)
XLA Modules:
  0.0 68.2 jit_solution(11890485651790627011)
XLA Ops:
  0.6 65.7 %shard_map.76 = (f32[1,128,512]{2,1,0:T(8,128)S(1)}, f32[4,256]{1,0:T(4,128)S(1)}, f32[4,256]{1,0:T(4,128)S(1)}) custom-call(s32[4]{0:T(128)} %len_hbm.1, bf16[1,128,4096]{2,1,0:T(8,128)(2,1)} %q_hbm.1, bf16[1,128,4096]{2,1,0:T(8,128)(2,1)} %g_hbm.1, bf16[4,256]{1,0:T(4,128)(2,1)} %k_hbm.1, bf16[4,256]{1,0:T(4,128)(2,1)} %v_hbm.1), custom_call_target="tpu_custom_call" | custom-call | tf_op jit(solution)/shard_map/pallas_call | solution.py:358
  66.3 0.7 %copy.11 = f32[1,128,512]{2,1,0:T(8,128)} copy(f32[1,128,512]{2,1,0:T(8,128)S(1)} %get-tuple-element.6) | data formatting | bytes 524288
  67.0 0.6 copy.12
  67.6 0.6 copy.13
